TPU v7x, 32 devices: a whole 2x2x4 slice. The times are simulated.
32 devices in a mesh: rot: 8 (over z, y), fft: 4 (over x, core).
Axes of the slice: x: 2, y: 2, z: 4, core: 2. Of those that a mesh axis runs over, the one named last changes fastest.
Arguments:
- receptor: bfloat16 [2, 11, 128, 128, 128], P(None, None, 'fft'), may hold values from -6 to 6, as said below
- ligand_grids: bfloat16 [32, 11, 32, 1024], P(None, None, 'fft'), may hold values from -8 to 8
- rot_index: int32 [48], P('rot'), parts along dimension 0, may hold values from 0 to 31
Outputs:
- scores: float32 [48, 128, 128, 128], P('rot', 'fft'), parts along dimension 0
- best: float32 [48], P('rot'), parts along dimension 0
There are 8 independent parts, one for each index of `rot`. A program takes and returns all parts, laid end to end along the dimension named above; an argument that names none is the same for every part. Nothing has to cross between parts.
Inputs may be any that keep to these rules, and one draw needn't show every extreme that they name: The receptor spectra are those of real grids: in every channel the entry at frequency (-kz, -kx, -ky), taken modulo 128 along each dimension, is the complex conjugate of the entry at (kz, kx, ky).
All inputs are finite; a program needn't handle non-finite values.
Results may differ from a plain program's by a relative error of at most 0.0003.
Values may be sent and summed in bfloat16 or wider, within the bound.
A program may use at most 256 MiB of HBM per device.

v0:
```python
import functools
import math

import jax
import jax.numpy as jnp
import ml_dtypes
import numpy as np
from jax import lax
from jax.experimental import pallas as pl
from jax.experimental.pallas import tpu as pltpu
from jax.sharding import PartitionSpec as P

BF = jnp.bfloat16
F32 = jnp.float32
TOP = 32767.0
LEVELS = 256.0


def halves(table):
    upper = table.astype(np.float32).astype(ml_dtypes.bfloat16)
    lower = (table - upper.astype(np.float64)).astype(np.float32)
    return upper, lower.astype(ml_dtypes.bfloat16)


def trig(rows, cols, length):
    angle = (np.outer(rows, cols) % length) * (2.0 * math.pi / length)
    return np.cos(angle), np.sin(angle)


def split(values):
    upper = values.astype(BF)
    return upper, (values - upper.astype(F32)).astype(BF)


def mul(left, right):
    return jnp.dot(left, right, preferred_element_type=F32)


def mul_t(left, right):
    return lax.dot_general(left, right, (((1,), (1,)), ((), ())), preferred_element_type=F32)


def up(value, step):
    return -(-value // step) * step


def pick_kernel(channels, block, index_ref, in_ref, out_ref):
    depth = in_ref.shape[2]
    parts = [in_ref[0, c].astype(F32) for c in range(channels)]
    if block > channels * depth:
        parts.append(jnp.zeros((block - channels * depth, in_ref.shape[3]), F32))
    out_ref[0] = jnp.concatenate(parts, axis=0).astype(BF)


def main_kernel(
    channels, planes, box, groups, rotations, length, block, rows,
    rec_hbm, own_hbm, tz_hbm, wy_ref, tx_ref, ti_ref, recv_hbm,
    rec, lbuf, tz, a_buf, b_re, b_im, qbuf,
    load_sem, own_sem, gsend, grecv, xsend, xrecv, self_sem,
):
    me = lax.axis_index("fft")
    xs = length // groups
    sib = me + 1 - 2 * lax.rem(me, 2)
    far = [lax.rem(me + 2 * m, groups) for m in range(1, groups // 2)]
    peers = [sib] + far
    others = [lax.rem(me + s, groups) for s in range(1, groups)]
    half = length // 2

    rec_copy = pltpu.make_async_copy(rec_hbm.at[:, :, pl.ds(0, planes)], rec, load_sem.at[0])
    rec_copy.start()
    tz_copy = pltpu.make_async_copy(tz_hbm.at[me], tz, load_sem.at[1])
    tz_copy.start()

    barrier = pltpu.get_barrier_semaphore()
    for peer in others:
        pl.semaphore_signal(barrier, inc=1, device_id={"fft": peer}, device_id_type=pl.DeviceIdType.MESH)
    pl.semaphore_wait(barrier, groups - 1)

    def slot(r, source):
        return lbuf.at[r, pl.ds(pl.multiple_of(source * block, block), block)]

    def own_copy(r, k):
        return pltpu.make_async_remote_copy(
            src_ref=own_hbm.at[r], dst_ref=slot(r, me), send_sem=gsend.at[r, k], recv_sem=grecv.at[r, me],
            device_id={"fft": peers[k]}, device_id_type=pl.DeviceIdType.MESH)

    def relay_copy(r, k):
        return pltpu.make_async_remote_copy(
            src_ref=slot(r, far[k]), dst_ref=slot(r, far[k]), send_sem=gsend.at[r, len(peers) + k],
            recv_sem=grecv.at[r, far[k]], device_id={"fft": sib}, device_id_type=pl.DeviceIdType.MESH)

    def arrival(r, source):
        return pltpu.make_async_remote_copy(
            src_ref=own_hbm.at[r], dst_ref=slot(r, source), send_sem=gsend.at[r, 0], recv_sem=grecv.at[r, source],
            device_id={"fft": sib}, device_id_type=pl.DeviceIdType.MESH)

    def local(r):
        return pltpu.make_async_copy(own_hbm.at[r], slot(r, me), own_sem.at[r])

    def begin(r):
        for k in range(len(peers)):
            own_copy(r, k).start()
        local(r).start()

    def relay(r):
        for k in range(len(far)):
            arrival(r, far[k]).wait_recv()
            relay_copy(r, k).start()

    def finish(r):
        arrival(r, sib).wait_recv()
        for m in range(1, groups // 2):
            arrival(r, lax.rem(sib + 2 * m, groups)).wait_recv()
        local(r).wait()

    def send_plane(r, k, s):
        peer = others[s]
        return pltpu.make_async_remote_copy(
            src_ref=qbuf.at[r, k, peer], dst_ref=recv_hbm.at[r, me, k],
            send_sem=xsend.at[r, s], recv_sem=xrecv.at[r, me],
            device_id={"fft": peer}, device_id_type=pl.DeviceIdType.MESH)

    def send_all(r, s):
        peer = others[s]
        return pltpu.make_async_remote_copy(
            src_ref=qbuf.at[r, :, peer], dst_ref=recv_hbm.at[r, peer],
            send_sem=xsend.at[r, s], recv_sem=xrecv.at[r, peer],
            device_id={"fft": peer}, device_id_type=pl.DeviceIdType.MESH)

    def keep(r):
        return pltpu.make_async_copy(
            qbuf.at[r, :, me], recv_hbm.at[r, me], self_sem.at[r])

    lanes = lax.broadcasted_iota(jnp.int32, (length, length), 1)

    def forward(r):
        finish(r)
        cells = lbuf[r]
        a_buf[...] = mul(tz[0], cells) + mul(tz[1], cells)

        @pl.when(r + 1 < rotations)
        def _():
            relay(r + 1)

        @pl.when(r + 2 < rotations)
        def _():
            begin(r + 2)

        def lane_group(j, carry):
            at = pl.ds(pl.multiple_of(j * 128, 128), 128)
            upper, lower = split(jnp.concatenate([a_buf[0:rows, at], a_buf[rows : 2 * rows, at]], axis=1))
            both = jnp.concatenate([upper, lower, upper], axis=1)
            per = 128 // box
            for i in range(per):
                out = mul(both, wy_ref[i])
                b_re[pl.ds(j * per + i, rows, stride=box), :] = out[:, :length]
                b_im[pl.ds(j * per + i, rows, stride=box), :] = out[:, length:]
            return carry

        lax.fori_loop(0, box * box // 128, lane_group, 0)

        @pl.when(r == 0)
        def _():
            rec_copy.wait()

        def plane(k, expo):
            p_re = p_im = None
            for c0 in range(0, channels, 2):
                pair = range(c0, min(c0 + 2, channels))
                at = [pl.ds(pl.multiple_of((k * channels + c) * box, box), box) for c in pair]
                re_hi, re_lo = split(jnp.concatenate([b_re[a, :] for a in at], axis=1))
                im_hi, im_lo = split(jnp.concatenate([b_im[a, :] for a in at], axis=1))
                spec = mul(tx_ref[...], jnp.concatenate([re_hi, im_hi, re_lo, im_lo, re_hi, im_hi], axis=0))
                for t, c in enumerate(pair):
                    s_re = spec[:length, t * length : (t + 1) * length]
                    s_im = spec[length:, t * length : (t + 1) * length]
                    r_re = rec[0, c, k].astype(F32)
                    r_im = rec[1, c, k].astype(F32)
                    q_re = r_re * s_re + r_im * s_im
                    q_im = r_im * s_re - r_re * s_im
                    p_re = q_re if p_re is None else p_re + q_re
                    p_im = q_im if p_im is None else p_im + q_im
            re_hi, re_lo = split(p_re)
            im_hi, im_lo = split(p_im)
            def square(re, im):
                return jnp.concatenate(
                    [jnp.concatenate([re, im], axis=1), jnp.concatenate([-im, re], axis=1)], axis=0)
            first = mul(ti_ref[...], square(re_hi, im_hi))
            field = first[:length] + first[length:] + mul(ti_ref[0:length], square(re_lo, im_lo))
            most = jnp.max(jnp.abs(field), axis=1, keepdims=True)
            code = jnp.ceil(LEVELS * jnp.log2(jnp.maximum(most, 1e-30))) + 1.0
            factor = TOP * jnp.exp2(code * (-1.0 / LEVELS))
            qbuf[r, k] = jnp.round(field * factor).astype(jnp.int32).reshape(groups, xs, 2 * length).astype(jnp.int16)
            for s in range(groups - 1):
                send_plane(r, k, s).start()
            return jnp.where(lanes == k, code, expo)

        expo = lax.fori_loop(0, planes, plane, jnp.zeros((length, length), F32))
        codes = jnp.concatenate([expo, expo], axis=1).astype(jnp.int32)
        qbuf[r, planes] = codes.reshape(groups, xs, 2 * length).astype(jnp.int16)
        for s in range(groups - 1):
            send_plane(r, planes, s).start()
        keep(r).start()

    begin(0)
    if rotations > 1:
        begin(1)
    tz_copy.wait()
    relay(0)

    def rotation(r, carry):
        forward(r)
        return carry

    lax.fori_loop(0, rotations, rotation, 0)

    def drain(r, carry):
        for k in range(len(peers)):
            own_copy(r, k).wait_send()
        for k in range(len(far)):
            relay_copy(r, k).wait_send()
        for s in range(groups - 1):
            send_all(r, s).wait_send()
            send_all(r, s).wait_recv()
        keep(r).wait()
        return carry

    lax.fori_loop(0, rotations, drain, 0)


def final_kernel(groups, planes, length, width, terms, blocks_ref, tz_ref, tw_ref, out_ref, low_ref, f_re, f_im):
    for s in range(groups):
        code = blocks_ref[0, s, planes].astype(jnp.int32).astype(F32)[:, :length]
        scale = jnp.exp2(code * (1.0 / LEVELS)) * (1.0 / TOP)
        for k in range(planes):
            value = blocks_ref[0, s, k].astype(jnp.int32).astype(F32) * scale[:, k : k + 1]
            at = pl.ds((s * planes + k) * width, width)
            f_re[at, :] = value[:, :length]
            f_im[at, :] = value[:, length:]
    if terms > groups * planes:
        rest = pl.ds(groups * planes * width, (terms - groups * planes) * width)
        f_re[rest, :] = jnp.zeros(((terms - groups * planes) * width, length), F32)
        f_im[rest, :] = jnp.zeros(((terms - groups * planes) * width, length), F32)
    for i in range(width):
        at = pl.ds(i, terms, stride=width)
        upper, lower = split(jnp.concatenate([f_re[at, :], f_im[at, :]], axis=1))
        both = mul(tz_ref[...], jnp.concatenate([upper, lower, upper], axis=0))
        g_re = both[:length, :length] - both[length:, length:]
        g_im = both[:length, length:] + both[length:, :length]
        upper, lower = split(jnp.concatenate([g_re, g_im], axis=1))
        first = mul_t(tw_ref[...], upper)
        plane = first[:length] + first[length:] + mul_t(tw_ref[0:length], lower)
        out_ref[0, i] = plane
        low_ref[0, 0, i : i + 1, :] = jnp.min(plane, axis=0, keepdims=True)


def shards(receptor, ligand_grids, rot_index):
    groups = lax.axis_size("fft")
    channels, slab, length = receptor.shape[1], receptor.shape[2], receptor.shape[3]
    depth = ligand_grids.shape[2]
    box = depth * groups
    cells = ligand_grids.shape[3]
    rotations = rot_index.shape[0]
    xs = length // groups
    planes = slab // 2 + 1
    block = up(channels * depth, 16)
    rows = up(planes * channels, 16)
    freq = np.arange(length)

    t_z = np.zeros((groups, 2, rows, groups, block))
    for d in range(groups):
        cz, sz = trig(d * slab + np.arange(planes), np.arange(box), length)
        for c in range(channels):
            at = np.arange(planes) * channels + c
            for s in range(groups):
                span = slice(c * depth, (c + 1) * depth)
                cut = slice(s * depth, (s + 1) * depth)
                t_z[d, 0, at, s, span] = cz[:, cut]
                t_z[d, 1, at, s, span] = -sz[:, cut]
    t_z = t_z.reshape(groups, 2 * rows, groups * block)
    t_z = jnp.asarray(np.stack(halves(t_z), axis=1))

    cy, sy = trig(np.arange(box), freq, length)
    per = 128 // box
    w_y = np.zeros((per, 256, 2 * length))
    for i in range(per):
        w_y[i, i * box : (i + 1) * box] = np.concatenate([cy, -sy], axis=1)
        w_y[i, 128 + i * box : 128 + (i + 1) * box] = np.concatenate([sy, cy], axis=1)
    hi, lo = halves(w_y)
    w_y = jnp.asarray(np.concatenate([hi, hi, lo], axis=1))

    t_x = np.block([[cy.T, sy.T], [-sy.T, cy.T]])
    hi, lo = halves(t_x)
    t_x = jnp.asarray(np.concatenate([hi, hi, lo], axis=1))

    cf, sf = trig(freq, freq, length)
    t_i = jnp.asarray(np.concatenate(halves(np.concatenate([cf, sf], axis=1)), axis=0))

    terms = up(groups * planes, 16)
    kz = np.zeros(terms, np.int64)
    weight = np.zeros(terms)
    for d in range(groups):
        for k in range(planes):
            f = d * slab + k
            kz[d * planes + k] = f
            if d < groups // 2:
                used = k < slab // 2
            else:
                used = k > 0 or f == length // 2
            weight[d * planes + k] = 0.0 if not used else 1.0 if f in (0, length // 2) else 2.0
    cb, sb = trig(freq, kz, length)
    hi, lo = halves(np.concatenate([cb * weight, sb * weight], axis=0))
    t_b = jnp.asarray(np.concatenate([hi, hi, lo], axis=1))
    t_w = jnp.asarray(np.concatenate(halves(np.concatenate([cf, -sf], axis=1) / float(length) ** 3), axis=0))

    own = pl.pallas_call(
        functools.partial(pick_kernel, channels, block),
        grid_spec=pltpu.PrefetchScalarGridSpec(
            num_scalar_prefetch=1,
            grid=(rotations,),
            in_specs=[pl.BlockSpec((1, channels, depth, cells), lambda r, index: (index[r], 0, 0, 0))],
            out_specs=pl.BlockSpec((1, block, cells), lambda r, index: (r, 0, 0)),
        ),
        out_shape=jax.ShapeDtypeStruct((rotations, block, cells), BF),
    )(rot_index, ligand_grids)

    any_space = pl.BlockSpec(memory_space=pl.ANY)
    vmem = pl.BlockSpec(memory_space=pltpu.VMEM)
    sent = pl.pallas_call(
        functools.partial(main_kernel, channels, planes, box, groups, rotations, length, block, rows),
        in_specs=[any_space, any_space, any_space, vmem, vmem, vmem],
        out_specs=any_space,
        out_shape=jax.ShapeDtypeStruct((rotations, groups, planes + 1, xs, 2 * length), jnp.int16),
        scratch_shapes=[
            pltpu.VMEM((2, channels, planes, length, length), BF),
            pltpu.VMEM((rotations, groups * block, cells), BF),
            pltpu.VMEM((2, 2 * rows, groups * block), BF),
            pltpu.VMEM((2 * rows, cells), F32),
            pltpu.VMEM((rows * box, length), F32),
            pltpu.VMEM((rows * box, length), F32),
            pltpu.VMEM((rotations, planes + 1, groups, xs, 2 * length), jnp.int16),
            pltpu.SemaphoreType.DMA((2,)),
            pltpu.SemaphoreType.DMA((rotations,)),
            pltpu.SemaphoreType.DMA((rotations, groups)),
            pltpu.SemaphoreType.DMA((rotations, groups)),
            pltpu.SemaphoreType.DMA((rotations, groups)),
            pltpu.SemaphoreType.DMA((rotations, groups)),
            pltpu.SemaphoreType.DMA((rotations,)),
        ],
        compiler_params=pltpu.CompilerParams(
            collective_id=0, has_side_effects=True, vmem_limit_bytes=56 * 2**20),
        cost_estimate=pl.CostEstimate(flops=rotations * 6 * 10**9, bytes_accessed=30_000_000, transcendentals=0),
    )(receptor, own, t_z, w_y, t_x, t_i)

    width = min(16, xs)
    scores, lows = pl.pallas_call(
        functools.partial(final_kernel, groups, planes, length, width, terms),
        grid=(rotations, xs // width),
        in_specs=[
            pl.BlockSpec((1, groups, planes + 1, width, 2 * length), lambda r, x: (r, 0, 0, x, 0)),
            pl.BlockSpec(t_b.shape, lambda r, x: (0, 0)),
            pl.BlockSpec(t_w.shape, lambda r, x: (0, 0)),
        ],
        out_specs=[
            pl.BlockSpec((1, width, length, length), lambda r, x: (r, x, 0, 0)),
            pl.BlockSpec((1, 1, width, length), lambda r, x: (r, x, 0, 0)),
        ],
        out_shape=[
            jax.ShapeDtypeStruct((rotations, xs, length, length), F32),
            jax.ShapeDtypeStruct((rotations, xs // width, width, length), F32),
        ],
        scratch_shapes=[pltpu.VMEM((terms * width, length), F32)] * 2,
        compiler_params=pltpu.CompilerParams(vmem_limit_bytes=32 * 2**20),
        cost_estimate=pl.CostEstimate(flops=rotations * 10**9, bytes_accessed=20_000_000, transcendentals=0),
    )(sent, t_b, t_w)
    best = lax.pmin(jnp.min(lows, axis=(1, 2, 3)), "fft")
    return scores, best


def solution(mesh):
    placed = (P(None, None, "fft", None, None), P(None, None, "fft", None), P("rot"))
    return jax.shard_map(
        shards,
        mesh=mesh,
        in_specs=placed,
        out_specs=(P("rot", "fft", None, None), P("rot")),
        check_vma=False,
    )
```

profile of v0, /device:TPU:0, one launch (start us, length us, event | category | flops | bytes accessed | tf_op | source)
XLA Modules:
  0.0 200.5 jit_solution(9347811797852806822)
XLA Ops:
  0.6 5.0 %shard_map.104.own_hbm = bf16[6,96,1024]{2,1,0:T(8,128)(2,1)} custom-call(s32[6]{0:T(128)} %index_ref.1, bf16[32,11,8,1024]{3,2,1,0:T(8,128)(2,1)} %in_ref.1), custom_call_target="tpu_custom_call" | custom-call | tf_op jit(solution)/shard_map/pallas_call | solution.py:316
  5.7 0.0 copy-start
  5.7 0.0 copy-start.1
  5.7 146.9 %shard_map.105.blocks_ref = s16[6,4,18,32,256]{4,3,2,1,0:T(8,128)(2,1)} custom-call(bf16[2,11,32,128,128]{4,3,2,1,0:T(8,128)(2,1)} %rec_hbm.1, bf16[6,96,1024]{2,1,0:T(8,128)(2,1)} %shard_map.104.own_hbm, bf16[4,2,384,384]{3,2,1,0:T(8,128)(2,1)} %constant.14.clone.tz_hbm, bf16[4,768,256]{2,1,0:T(8,128)(2,1)} %constant.15.clone.wy_ref, ...), custom_call_target="tpu_custom_call" | custom-call | flops 35999997952 | bytes 30000000 | tf_op jit(solution)/shard_map/pallas_call | solution.py:329
  152.6 0.0 copy-done
  152.6 0.0 copy-done.1
  152.6 0.0 copy-start.2
  152.6 3.0 %copy-done.2 = s16[6,4,18,32,256]{4,3,2,1,0:T(8,128)(2,1)S(1)} copy-done((s16[6,4,18,32,256]{4,3,2,1,0:T(8,128)(2,1)S(1)}, s16[6,4,18,32,256]{4,3,2,1,0:T(8,128)(2,1)}, u32[]{:S(2)}) %copy-start.2) | copy-done | bytes 7077912
  155.6 38.3 %shard_map.106 = (f32[6,32,128,128]{3,2,1,0:T(8,128)}, f32[6,2,16,128]{3,2,1,0:T(8,128)S(1)}) custom-call(s16[6,4,18,32,256]{4,3,2,1,0:T(8,128)(2,1)S(1)} %copy-done.2, bf16[256,240]{1,0:T(8,128)(2,1)S(1)} %copy-done.1, bf16[256,256]{1,0:T(8,128)(2,1)S(1)} %copy-done), custom_call_target="tpu_custom_call" | custom-call | flops 6000000000 | bytes 20000000 | tf_op jit(solution)/shard_map/pallas_call | solution.py:356
  193.8 0.1 reduce_min.9
  194.0 6.5 %pmin.7 = f32[6]{0:T(128)} all-reduce(f32[6]{0:T(128)S(1)} %reduce_min.9), channel_id=1, replica_groups=mesh['rot'=8,'fft'=4] {'fft'}, use_global_device_ids=true, to_apply=%region_1.0 | all-reduce | flops 6 | bytes 48 | tf_op jit(solution)/shard_map/pmin | solution.py:376
Async XLA Ops:
  5.7 146.9 %copy-start = (bf16[256,256]{1,0:T(8,128)(2,1)S(1)}, bf16[256,256]{1,0:T(8,128)(2,1)}, u32[]{:S(2)}) copy-start(bf16[256,256]{1,0:T(8,128)(2,1)} %constant.19.clone.tw_ref) | copy-start | bytes 393220
  5.7 146.9 %copy-start.1 = (bf16[256,240]{1,0:T(8,128)(2,1)S(1)}, bf16[256,240]{1,0:T(8,128)(2,1)}, u32[]{:S(2)}) copy-start(bf16[256,240]{1,0:T(8,128)(2,1)} %constant.18.clone.tz_ref) | copy-start | bytes 368644
  152.6 3.0 %copy-start.2 = (s16[6,4,18,32,256]{4,3,2,1,0:T(8,128)(2,1)S(1)}, s16[6,4,18,32,256]{4,3,2,1,0:T(8,128)(2,1)}, u32[]{:S(2)}) copy-start(s16[6,4,18,32,256]{4,3,2,1,0:T(8,128)(2,1)} %shard_map.105.blocks_ref) | copy-start | bytes 21233668
where the time goes:
time: 201 us; the launch traced here: 200 us
  Pallas kernels  190 us (95%)
  blocking collectives  6.49 us (3%)
  local copies, waits for them, and re-layouts  3.01 us (1%)
    pallas_call x1, Pallas kernels, shards(): pl.pallas_call(functools.partial(main_kernel, channels, planes, box, grou...  147 us
    pallas_call x1, Pallas kernels, shards(): pl.pallas_call(functools.partial(final_kernel, groups, planes, length, wi...  38.3 us
    pmin x1, blocking collectives, shards(): best = lax.pmin(jnp.min(lows, axis=(1, 2, 3)), 'fft')  6.49 us
    pallas_call x1, Pallas kernels, shards(): pl.pallas_call(functools.partial(pick_kernel, channels, block), grid_spec...  5.03 us

commit v1 on v0

--- a/solution.py
+++ b/solution.py
@@ -55,7 +55,7 @@
 def main_kernel(
     channels, planes, box, groups, rotations, length, block, rows,
     rec_hbm, own_hbm, tz_hbm, wy_ref, tx_ref, ti_ref, recv_hbm,
-    rec, lbuf, tz, a_buf, b_re, b_im, qbuf,
+    rec, lbuf, tz, a_buf, b_re, b_im, spec_a, spec_b, square_a, square_b, expo, qbuf,
     load_sem, own_sem, gsend, grecv, xsend, xrecv, self_sem,
 ):
     me = lax.axis_index("fft")
@@ -64,7 +64,7 @@
     far = [lax.rem(me + 2 * m, groups) for m in range(1, groups // 2)]
     peers = [sib] + far
     others = [lax.rem(me + s, groups) for s in range(1, groups)]
-    half = length // 2
+    pairs = -(-channels // 2)
 
     rec_copy = pltpu.make_async_copy(rec_hbm.at[:, :, pl.ds(0, planes)], rec, load_sem.at[0])
     rec_copy.start()
@@ -153,8 +153,10 @@
             per = 128 // box
             for i in range(per):
                 out = mul(both, wy_ref[i])
-                b_re[pl.ds(j * per + i, rows, stride=box), :] = out[:, :length]
-                b_im[pl.ds(j * per + i, rows, stride=box), :] = out[:, length:]
+                for g in range(rows // 8):
+                    to = pl.ds(pl.multiple_of((g * box + j * per + i) * 8, 8), 8)
+                    b_re[to, :] = out[g * 8 : g * 8 + 8, :length]
+                    b_im[to, :] = out[g * 8 : g * 8 + 8, length:]
             return carry
 
         lax.fori_loop(0, box * box // 128, lane_group, 0)
@@ -163,43 +165,80 @@
         def _():
             rec_copy.wait()
 
-        def plane(k, expo):
-            p_re = p_im = None
-            for c0 in range(0, channels, 2):
-                pair = range(c0, min(c0 + 2, channels))
-                at = [pl.ds(pl.multiple_of((k * channels + c) * box, box), box) for c in pair]
-                re_hi, re_lo = split(jnp.concatenate([b_re[a, :] for a in at], axis=1))
-                im_hi, im_lo = split(jnp.concatenate([b_im[a, :] for a in at], axis=1))
-                spec = mul(tx_ref[...], jnp.concatenate([re_hi, im_hi, re_lo, im_lo, re_hi, im_hi], axis=0))
-                for t, c in enumerate(pair):
-                    s_re = spec[:length, t * length : (t + 1) * length]
-                    s_im = spec[length:, t * length : (t + 1) * length]
-                    r_re = rec[0, c, k].astype(F32)
-                    r_im = rec[1, c, k].astype(F32)
+        def x_stage(k, spec):
+            for p in range(pairs):
+                pair = range(2 * p, min(2 * p + 2, channels))
+                def pick(ref):
+                    parts = []
+                    for c in pair:
+                        row = k * channels + c
+                        parts.append(ref[pl.ds(row // 8 * (box * 8) + lax.rem(row, 8), box, stride=8), :])
+                    return split(jnp.concatenate(parts, axis=1))
+                re_hi, re_lo = pick(b_re)
+                im_hi, im_lo = pick(b_im)
+                right = jnp.concatenate([re_hi, im_hi, re_lo, im_lo, re_hi, im_hi], axis=0)
+                spec[p, :, 0 : length * len(pair)] = mul(tx_ref[...], right)
+
+        def product(k, spec, square):
+            for h in range(0, length, 16):
+                low, high = slice(h, h + 16), slice(length + h, length + h + 16)
+                p_re = p_im = None
+                for c in range(channels):
+                    at = slice((c % 2) * length, (c % 2 + 1) * length)
+                    s_re = spec[c // 2, low, at]
+                    s_im = spec[c // 2, high, at]
+                    r_re = rec[0, c, k, low].astype(F32)
+                    r_im = rec[1, c, k, low].astype(F32)
                     q_re = r_re * s_re + r_im * s_im
                     q_im = r_im * s_re - r_re * s_im
                     p_re = q_re if p_re is None else p_re + q_re
                     p_im = q_im if p_im is None else p_im + q_im
-            re_hi, re_lo = split(p_re)
-            im_hi, im_lo = split(p_im)
-            def square(re, im):
-                return jnp.concatenate(
-                    [jnp.concatenate([re, im], axis=1), jnp.concatenate([-im, re], axis=1)], axis=0)
-            first = mul(ti_ref[...], square(re_hi, im_hi))
-            field = first[:length] + first[length:] + mul(ti_ref[0:length], square(re_lo, im_lo))
+                for t, (re, im) in enumerate(zip(split(p_re), split(p_im))):
+                    square[t, low, 0:length] = re
+                    square[t, low, length : 2 * length] = im
+                    square[t, high, 0:length] = -im
+                    square[t, high, length : 2 * length] = re
+
+        def close(k, square):
+            upper = square[0]
+            field = mul(ti_ref[...], jnp.concatenate([upper, upper, square[1]], axis=0))
             most = jnp.max(jnp.abs(field), axis=1, keepdims=True)
             code = jnp.ceil(LEVELS * jnp.log2(jnp.maximum(most, 1e-30))) + 1.0
             factor = TOP * jnp.exp2(code * (-1.0 / LEVELS))
             qbuf[r, k] = jnp.round(field * factor).astype(jnp.int32).reshape(groups, xs, 2 * length).astype(jnp.int16)
+            expo[...] = jnp.where(lanes == k, code, expo[...])
+
+        def send(k):
             for s in range(groups - 1):
                 send_plane(r, k, s).start()
-            return jnp.where(lanes == k, code, expo)
-
-        expo = lax.fori_loop(0, planes, plane, jnp.zeros((length, length), F32))
-        codes = jnp.concatenate([expo, expo], axis=1).astype(jnp.int32)
+
+        def two(m, carry):
+            k = 2 * m
+            x_stage(k - 1, spec_b)
+            product(k - 2, spec_a, square_a)
+            close(jnp.maximum(k - 3, 0), square_b)
+            x_stage(k, spec_a)
+            product(k - 1, spec_b, square_b)
+            close(k - 2, square_a)
+
+            @pl.when(m > 1)
+            def _():
+                send(k - 3)
+
+            send(k - 2)
+            return carry
+
+        x_stage(0, spec_a)
+        lax.fori_loop(1, planes // 2 + 1, two, 0)
+        product(planes - 1, spec_a, square_a)
+        close(planes - 2, square_b)
+        close(planes - 1, square_a)
+        send(planes - 2)
+        send(planes - 1)
+        codes = expo[...].astype(jnp.int32)
+        codes = jnp.concatenate([codes, codes], axis=1)
         qbuf[r, planes] = codes.reshape(groups, xs, 2 * length).astype(jnp.int16)
-        for s in range(groups - 1):
-            send_plane(r, planes, s).start()
+        send(planes)
         keep(r).start()
 
     begin(0)
@@ -294,7 +333,8 @@
     t_x = jnp.asarray(np.concatenate([hi, hi, lo], axis=1))
 
     cf, sf = trig(freq, freq, length)
-    t_i = jnp.asarray(np.concatenate(halves(np.concatenate([cf, sf], axis=1)), axis=0))
+    hi, lo = halves(np.concatenate([cf, sf], axis=1))
+    t_i = jnp.asarray(np.concatenate([hi, lo, hi], axis=1))
 
     terms = up(groups * planes, 16)
     kz = np.zeros(terms, np.int64)
@@ -338,6 +378,11 @@
             pltpu.VMEM((2 * rows, cells), F32),
             pltpu.VMEM((rows * box, length), F32),
             pltpu.VMEM((rows * box, length), F32),
+            pltpu.VMEM((-(-channels // 2), 2 * length, 2 * length), F32),
+            pltpu.VMEM((-(-channels // 2), 2 * length, 2 * length), F32),
+            pltpu.VMEM((2, 2 * length, 2 * length), BF),
+            pltpu.VMEM((2, 2 * length, 2 * length), BF),
+            pltpu.VMEM((length, length), F32),
             pltpu.VMEM((rotations, planes + 1, groups, xs, 2 * length), jnp.int16),
             pltpu.SemaphoreType.DMA((2,)),
             pltpu.SemaphoreType.DMA((rotations,)),

time: 201 us -> 168 us (0.84)
  Pallas kernels: 190 us -> 158 us
    pallas_call x1, Pallas kernels: 147 us -> 114 us  [shards(): pl.pallas_call(functools.partial(main_kernel, channels, planes, box, grou...]
where the time goes in v1:
time: 168 us
  Pallas kernels  158 us (94%)
  blocking collectives  6.28 us (4%)
  local copies, waits for them, and re-layouts  3.01 us (2%)
    pallas_call x1, Pallas kernels, shards(): pl.pallas_call(functools.partial(main_kernel, channels, planes, box, grou...  114 us
    pallas_call x1, Pallas kernels, shards(): pl.pallas_call(functools.partial(final_kernel, groups, planes, length, wi...  38.3 us
    pmin x1, blocking collectives, shards(): best = lax.pmin(jnp.min(lows, axis=(1, 2, 3)), 'fft')  6.28 us
    pallas_call x1, Pallas kernels, shards(): pl.pallas_call(functools.partial(pick_kernel, channels, block), grid_spec...  5.08 us

profile of v1, /device:TPU:0, one launch (start us, length us, event | category | flops | bytes accessed | tf_op | source)
XLA Modules:
  0.0 167.8 jit_solution(973319832879010350)
XLA Ops:
  0.6 5.1 %shard_map.104.own_hbm = bf16[6,96,1024]{2,1,0:T(8,128)(2,1)} custom-call(s32[6]{0:T(128)} %index_ref.1, bf16[32,11,8,1024]{3,2,1,0:T(8,128)(2,1)} %in_ref.1), custom_call_target="tpu_custom_call" | custom-call | tf_op jit(solution)/shard_map/pallas_call | solution.py:356
  5.7 0.0 copy-start
  5.7 0.0 copy-start.1
  5.7 114.4 %shard_map.105.blocks_ref = s16[6,4,18,32,256]{4,3,2,1,0:T(8,128)(2,1)} custom-call(bf16[2,11,32,128,128]{4,3,2,1,0:T(8,128)(2,1)} %rec_hbm.1, bf16[6,96,1024]{2,1,0:T(8,128)(2,1)} %shard_map.104.own_hbm, bf16[4,2,384,384]{3,2,1,0:T(8,128)(2,1)} %constant.14.clone.tz_hbm, bf16[4,768,256]{2,1,0:T(8,128)(2,1)} %constant.15.clone.wy_ref, ...), custom_call_target="tpu_custom_call" | custom-call | flops 35999997952 | bytes 30000000 | tf_op jit(solution)/shard_map/pallas_call | solution.py:369
  120.1 0.0 copy-done
  120.1 0.0 copy-done.1
  120.1 0.0 copy-start.2
  120.1 3.0 %copy-done.2 = s16[6,4,18,32,256]{4,3,2,1,0:T(8,128)(2,1)S(1)} copy-done((s16[6,4,18,32,256]{4,3,2,1,0:T(8,128)(2,1)S(1)}, s16[6,4,18,32,256]{4,3,2,1,0:T(8,128)(2,1)}, u32[]{:S(2)}) %copy-start.2) | copy-done | bytes 7077912
  123.1 38.3 %shard_map.106 = (f32[6,32,128,128]{3,2,1,0:T(8,128)}, f32[6,2,16,128]{3,2,1,0:T(8,128)S(1)}) custom-call(s16[6,4,18,32,256]{4,3,2,1,0:T(8,128)(2,1)S(1)} %copy-done.2, bf16[256,240]{1,0:T(8,128)(2,1)S(1)} %copy-done.1, bf16[256,256]{1,0:T(8,128)(2,1)S(1)} %copy-done), custom_call_target="tpu_custom_call" | custom-call | flops 6000000000 | bytes 20000000 | tf_op jit(solution)/shard_map/pallas_call | solution.py:401
  161.4 0.1 reduce_min.9
  161.5 6.3 %pmin.7 = f32[6]{0:T(128)} all-reduce(f32[6]{0:T(128)S(1)} %reduce_min.9), channel_id=1, replica_groups=mesh['rot'=8,'fft'=4] {'fft'}, use_global_device_ids=true, to_apply=%region_1.0 | all-reduce | flops 6 | bytes 48 | tf_op jit(solution)/shard_map/pmin | solution.py:421
Async XLA Ops:
  5.7 114.4 %copy-start = (bf16[256,256]{1,0:T(8,128)(2,1)S(1)}, bf16[256,256]{1,0:T(8,128)(2,1)}, u32[]{:S(2)}) copy-start(bf16[256,256]{1,0:T(8,128)(2,1)} %constant.19.clone.tw_ref) | copy-start | bytes 393220
  5.7 114.4 %copy-start.1 = (bf16[256,240]{1,0:T(8,128)(2,1)S(1)}, bf16[256,240]{1,0:T(8,128)(2,1)}, u32[]{:S(2)}) copy-start(bf16[256,240]{1,0:T(8,128)(2,1)} %constant.18.clone.tz_ref) | copy-start | bytes 368644
  120.1 3.0 %copy-start.2 = (s16[6,4,18,32,256]{4,3,2,1,0:T(8,128)(2,1)S(1)}, s16[6,4,18,32,256]{4,3,2,1,0:T(8,128)(2,1)}, u32[]{:S(2)}) copy-start(s16[6,4,18,32,256]{4,3,2,1,0:T(8,128)(2,1)} %shard_map.105.blocks_ref) | copy-start | bytes 21233668

commit v2 on v1

--- a/solution.py
+++ b/solution.py
@@ -267,30 +267,31 @@
     lax.fori_loop(0, rotations, drain, 0)
 
 
-def final_kernel(groups, planes, length, width, terms, blocks_ref, tz_ref, tw_ref, out_ref, low_ref, f_re, f_im):
+def final_kernel(groups, planes, length, width, terms, blocks_ref, ty_ref, tz_ref, out_ref, low_ref, h_re, h_im):
     for s in range(groups):
         code = blocks_ref[0, s, planes].astype(jnp.int32).astype(F32)[:, :length]
         scale = jnp.exp2(code * (1.0 / LEVELS)) * (1.0 / TOP)
-        for k in range(planes):
-            value = blocks_ref[0, s, k].astype(jnp.int32).astype(F32) * scale[:, k : k + 1]
-            at = pl.ds((s * planes + k) * width, width)
-            f_re[at, :] = value[:, :length]
-            f_im[at, :] = value[:, length:]
+        parts = [blocks_ref[0, s, k].astype(jnp.int32).astype(F32) * scale[:, k : k + 1] for k in range(planes)]
+        upper, lower = split(jnp.concatenate(parts, axis=0))
+        lines = mul(jnp.concatenate([upper, upper, lower], axis=1), ty_ref[...])
+        at = pl.ds(s * planes * width, planes * width)
+        h_re[at, :] = lines[:, :length]
+        h_im[at, :] = lines[:, length:]
     if terms > groups * planes:
         rest = pl.ds(groups * planes * width, (terms - groups * planes) * width)
-        f_re[rest, :] = jnp.zeros(((terms - groups * planes) * width, length), F32)
-        f_im[rest, :] = jnp.zeros(((terms - groups * planes) * width, length), F32)
-    for i in range(width):
-        at = pl.ds(i, terms, stride=width)
-        upper, lower = split(jnp.concatenate([f_re[at, :], f_im[at, :]], axis=1))
-        both = mul(tz_ref[...], jnp.concatenate([upper, lower, upper], axis=0))
-        g_re = both[:length, :length] - both[length:, length:]
-        g_im = both[:length, length:] + both[length:, :length]
-        upper, lower = split(jnp.concatenate([g_re, g_im], axis=1))
-        first = mul_t(tw_ref[...], upper)
-        plane = first[:length] + first[length:] + mul_t(tw_ref[0:length], lower)
-        out_ref[0, i] = plane
-        low_ref[0, 0, i : i + 1, :] = jnp.min(plane, axis=0, keepdims=True)
+        h_re[rest, :] = jnp.zeros(((terms - groups * planes) * width, length), F32)
+        h_im[rest, :] = jnp.zeros(((terms - groups * planes) * width, length), F32)
+    for i in range(0, width, 2):
+        def both(ref):
+            return split(jnp.concatenate([ref[pl.ds(i + t, terms, stride=width), :] for t in range(2)], axis=1))
+        re_hi, re_lo = both(h_re)
+        im_hi, im_lo = both(h_im)
+        right = jnp.concatenate([re_hi, im_hi, re_lo, im_lo, re_hi, im_hi], axis=0)
+        field = mul(tz_ref[...], right)
+        for t in range(2):
+            plane = field[:, t * length : (t + 1) * length]
+            low_ref[0, 0, i + t : i + t + 1, :] = jnp.min(plane, axis=0, keepdims=True)
+            out_ref[0, i + t] = plane.T
 
 
 def shards(receptor, ligand_grids, rot_index):
@@ -349,9 +350,10 @@
                 used = k > 0 or f == length // 2
             weight[d * planes + k] = 0.0 if not used else 1.0 if f in (0, length // 2) else 2.0
     cb, sb = trig(freq, kz, length)
-    hi, lo = halves(np.concatenate([cb * weight, sb * weight], axis=0))
+    hi, lo = halves(np.concatenate([cb * weight, -sb * weight], axis=1))
     t_b = jnp.asarray(np.concatenate([hi, hi, lo], axis=1))
-    t_w = jnp.asarray(np.concatenate(halves(np.concatenate([cf, -sf], axis=1) / float(length) ** 3), axis=0))
+    hi, lo = halves(np.block([[cf, sf], [-sf, cf]]) / float(length) ** 3)
+    t_w = jnp.asarray(np.concatenate([hi, lo, hi], axis=0))
 
     own = pl.pallas_call(
         functools.partial(pick_kernel, channels, block),
@@ -403,8 +405,8 @@
         grid=(rotations, xs // width),
         in_specs=[
             pl.BlockSpec((1, groups, planes + 1, width, 2 * length), lambda r, x: (r, 0, 0, x, 0)),
+            pl.BlockSpec(t_w.shape, lambda r, x: (0, 0)),
             pl.BlockSpec(t_b.shape, lambda r, x: (0, 0)),
-            pl.BlockSpec(t_w.shape, lambda r, x: (0, 0)),
         ],
         out_specs=[
             pl.BlockSpec((1, width, length, length), lambda r, x: (r, x, 0, 0)),
@@ -417,7 +419,7 @@
         scratch_shapes=[pltpu.VMEM((terms * width, length), F32)] * 2,
         compiler_params=pltpu.CompilerParams(vmem_limit_bytes=32 * 2**20),
         cost_estimate=pl.CostEstimate(flops=rotations * 10**9, bytes_accessed=20_000_000, transcendentals=0),
-    )(sent, t_b, t_w)
+    )(sent, t_w, t_b)
     best = lax.pmin(jnp.min(lows, axis=(1, 2, 3)), "fft")
     return scores, best
 

time: 168 us -> 149 us (0.89)
  Pallas kernels: 158 us -> 138 us
    pallas_call x1, Pallas kernels: 38.3 us -> 19.1 us  [shards(): pl.pallas_call(functools.partial(final_kernel, groups, planes, length, wi...]
where the time goes in v2:
time: 149 us
  Pallas kernels  138 us (93%)
  blocking collectives  6.25 us (4%)
  local copies, waits for them, and re-layouts  3.01 us (2%)
    pallas_call x1, Pallas kernels, shards(): pl.pallas_call(functools.partial(main_kernel, channels, planes, box, grou...  114 us
    pallas_call x1, Pallas kernels, shards(): pl.pallas_call(functools.partial(final_kernel, groups, planes, length, wi...  19.1 us
    pmin x1, blocking collectives, shards(): best = lax.pmin(jnp.min(lows, axis=(1, 2, 3)), 'fft')  6.25 us
    pallas_call x1, Pallas kernels, shards(): pl.pallas_call(functools.partial(pick_kernel, channels, block), grid_spec...  5.03 us
    unnamed x6, local copies, waits for them, and re-layouts  3.01 us

profile of v2, /device:TPU:0, one launch (start us, length us, event | category | flops | bytes accessed | tf_op | source)
XLA Modules:
  0.0 148.5 jit_solution(14907940025834861839)
XLA Ops:
  0.6 5.0 %shard_map.104.own_hbm = bf16[6,96,1024]{2,1,0:T(8,128)(2,1)} custom-call(s32[6]{0:T(128)} %index_ref.1, bf16[32,11,8,1024]{3,2,1,0:T(8,128)(2,1)} %in_ref.1), custom_call_target="tpu_custom_call" | custom-call | tf_op jit(solution)/shard_map/pallas_call | solution.py:358
  5.7 0.0 copy-start
  5.7 0.0 copy-start.1
  5.7 114.4 %shard_map.105.blocks_ref = s16[6,4,18,32,256]{4,3,2,1,0:T(8,128)(2,1)} custom-call(bf16[2,11,32,128,128]{4,3,2,1,0:T(8,128)(2,1)} %rec_hbm.1, bf16[6,96,1024]{2,1,0:T(8,128)(2,1)} %shard_map.104.own_hbm, bf16[4,2,384,384]{3,2,1,0:T(8,128)(2,1)} %constant.14.clone.tz_hbm, bf16[4,768,256]{2,1,0:T(8,128)(2,1)} %constant.15.clone.wy_ref, ...), custom_call_target="tpu_custom_call" | custom-call | flops 35999997952 | bytes 30000000 | tf_op jit(solution)/shard_map/pallas_call | solution.py:371
  120.1 0.0 copy-done
  120.1 0.0 copy-done.1
  120.1 0.0 copy-start.2
  120.1 3.0 %copy-done.2 = s16[6,4,18,32,256]{4,3,2,1,0:T(8,128)(2,1)S(1)} copy-done((s16[6,4,18,32,256]{4,3,2,1,0:T(8,128)(2,1)S(1)}, s16[6,4,18,32,256]{4,3,2,1,0:T(8,128)(2,1)}, u32[]{:S(2)}) %copy-start.2) | copy-done | bytes 7077912
  123.1 19.1 %shard_map.106 = (f32[6,32,128,128]{3,2,1,0:T(8,128)}, f32[6,2,16,128]{3,2,1,0:T(8,128)S(1)}) custom-call(s16[6,4,18,32,256]{4,3,2,1,0:T(8,128)(2,1)S(1)} %copy-done.2, bf16[768,256]{1,0:T(8,128)(2,1)S(1)} %copy-done, bf16[128,480]{1,0:T(8,128)(2,1)S(1)} %copy-done.1), custom_call_target="tpu_custom_call" | custom-call | flops 6000000000 | bytes 20000000 | tf_op jit(solution)/shard_map/pallas_call | solution.py:403
  142.2 0.1 reduce_min.9
  142.3 6.3 %pmin.7 = f32[6]{0:T(128)} all-reduce(f32[6]{0:T(128)S(1)} %reduce_min.9), channel_id=1, replica_groups=mesh['rot'=8,'fft'=4] {'fft'}, use_global_device_ids=true, to_apply=%region_1.0 | all-reduce | flops 6 | bytes 48 | tf_op jit(solution)/shard_map/pmin | solution.py:423
Async XLA Ops:
  5.7 114.4 %copy-start = (bf16[768,256]{1,0:T(8,128)(2,1)S(1)}, bf16[768,256]{1,0:T(8,128)(2,1)}, u32[]{:S(2)}) copy-start(bf16[768,256]{1,0:T(8,128)(2,1)} %constant.19.clone.ty_ref) | copy-start | bytes 1179652
  5.7 114.4 %copy-start.1 = (bf16[128,480]{1,0:T(8,128)(2,1)S(1)}, bf16[128,480]{1,0:T(8,128)(2,1)}, u32[]{:S(2)}) copy-start(bf16[128,480]{1,0:T(8,128)(2,1)} %constant.18.clone.tz_ref) | copy-start | bytes 368644
  120.1 3.0 %copy-start.2 = (s16[6,4,18,32,256]{4,3,2,1,0:T(8,128)(2,1)S(1)}, s16[6,4,18,32,256]{4,3,2,1,0:T(8,128)(2,1)}, u32[]{:S(2)}) copy-start(s16[6,4,18,32,256]{4,3,2,1,0:T(8,128)(2,1)} %shard_map.105.blocks_ref) | copy-start | bytes 21233668

commit v3 on v2

--- a/solution.py
+++ b/solution.py
@@ -44,21 +44,26 @@
     return -(-value // step) * step
 
 
-def pick_kernel(channels, block, index_ref, in_ref, out_ref):
-    depth = in_ref.shape[2]
-    parts = [in_ref[0, c].astype(F32) for c in range(channels)]
-    if block > channels * depth:
-        parts.append(jnp.zeros((block - channels * depth, in_ref.shape[3]), F32))
+def pick_kernel(cuts, index_ref, in_ref, out_ref):
+    depth, cells = in_ref.shape[2], in_ref.shape[3]
+    parts = []
+    for start, stop, size in cuts:
+        parts += [in_ref[0, c].astype(F32) for c in range(start, stop)]
+        if size > (stop - start) * depth:
+            parts.append(jnp.zeros((size - (stop - start) * depth, cells), F32))
     out_ref[0] = jnp.concatenate(parts, axis=0).astype(BF)
 
 
 def main_kernel(
-    channels, planes, box, groups, rotations, length, block, rows,
-    rec_hbm, own_hbm, tz_hbm, wy_ref, tx_ref, ti_ref, recv_hbm,
-    rec, lbuf, tz, a_buf, b_re, b_im, spec_a, spec_b, square_a, square_b, expo, qbuf,
+    channels, planes, box, groups, rotations, length, cuts, tops,
+    rec_hbm, own_hbm, tza_hbm, tzb_hbm, wy_ref, tx_ref, ti_ref, recv_hbm,
+    rec, stage, lbuf, tza, tzb, a_buf, even_re, even_im, odd_re, odd_im, spec_a, spec_b, square_a, square_b, expo, qbuf,
     load_sem, own_sem, gsend, grecv, xsend, xrecv, self_sem,
 ):
     me = lax.axis_index("fft")
+    block = cuts[0][2] + cuts[1][2]
+    rows = tops[0] + tops[1]
+    middle = cuts[1][0]
     xs = length // groups
     sib = me + 1 - 2 * lax.rem(me, 2)
     far = [lax.rem(me + 2 * m, groups) for m in range(1, groups // 2)]
@@ -66,10 +71,17 @@
     others = [lax.rem(me + s, groups) for s in range(1, groups)]
     pairs = -(-channels // 2)
 
-    rec_copy = pltpu.make_async_copy(rec_hbm.at[:, :, pl.ds(0, planes)], rec, load_sem.at[0])
-    rec_copy.start()
-    tz_copy = pltpu.make_async_copy(tz_hbm.at[me], tz, load_sem.at[1])
-    tz_copy.start()
+    def fetch(k):
+        slot_at = lax.rem(k, 2)
+        return pltpu.make_async_copy(rec_hbm.at[:, :, k], stage.at[slot_at], load_sem.at[slot_at])
+
+    fetch(0).start()
+    table_copies = [
+        pltpu.make_async_copy(tza_hbm.at[me], tza, load_sem.at[2]),
+        pltpu.make_async_copy(tzb_hbm.at[me], tzb, load_sem.at[3]),
+    ]
+    for copy in table_copies:
+        copy.start()
 
     barrier = pltpu.get_barrier_semaphore()
     for peer in others:
@@ -116,54 +128,79 @@
     def send_plane(r, k, s):
         peer = others[s]
         return pltpu.make_async_remote_copy(
-            src_ref=qbuf.at[r, k, peer], dst_ref=recv_hbm.at[r, me, k],
+            src_ref=qbuf.at[lax.rem(r, 2), k, peer], dst_ref=recv_hbm.at[r, me, k],
             send_sem=xsend.at[r, s], recv_sem=xrecv.at[r, me],
             device_id={"fft": peer}, device_id_type=pl.DeviceIdType.MESH)
 
     def send_all(r, s):
         peer = others[s]
         return pltpu.make_async_remote_copy(
-            src_ref=qbuf.at[r, :, peer], dst_ref=recv_hbm.at[r, peer],
+            src_ref=qbuf.at[lax.rem(r, 2), :, peer], dst_ref=recv_hbm.at[r, peer],
             send_sem=xsend.at[r, s], recv_sem=xrecv.at[r, peer],
             device_id={"fft": peer}, device_id_type=pl.DeviceIdType.MESH)
 
     def keep(r):
         return pltpu.make_async_copy(
-            qbuf.at[r, :, me], recv_hbm.at[r, me], self_sem.at[r])
+            qbuf.at[lax.rem(r, 2), :, me], recv_hbm.at[r, me], self_sem.at[r])
 
     lanes = lax.broadcasted_iota(jnp.int32, (length, length), 1)
 
-    def forward(r):
-        finish(r)
-        cells = lbuf[r]
-        a_buf[...] = mul(tz[0], cells) + mul(tz[1], cells)
+    per = 128 // box
+    lane_groups = box * box // 128
+
+    def z_stage(r):
+        for half, table in enumerate((tza, tzb)):
+            skip, size, top = half * cuts[0][2], cuts[half][2], tops[half]
+            cells = jnp.concatenate([lbuf[r, s * block + skip : s * block + skip + size] for s in range(groups)], axis=0)
+            out = mul(table[0], cells) + mul(table[1], cells)
+            to = half * tops[0]
+            a_buf[to : to + top] = out[:top]
+            a_buf[rows + to : rows + to + top] = out[top:]
+
+    first_lanes = lax.broadcasted_iota(jnp.int32, (rows, 128), 1) < 64
+
+    def lane_group(j, b_re, b_im):
+        at = pl.ds(pl.multiple_of(j * 128, 128), 128)
+        whole, early, late = [], [], []
+        for values in (a_buf[0:rows, at], a_buf[rows : 2 * rows, at]):
+            upper = values.astype(BF)
+            wide = upper.astype(F32)
+            lower = pltpu.roll(values - wide, 64, 1)
+            whole.append(upper)
+            early.append(jnp.where(first_lanes, wide, lower).astype(BF))
+            late.append(jnp.where(first_lanes, lower, wide).astype(BF))
+        for i in range(per):
+            out = mul(jnp.concatenate((early if i < per // 2 else late) + whole, axis=1), wy_ref[i])
+            for g in range(rows // 8):
+                to = pl.ds(pl.multiple_of((g * box + j * per + i) * 8, 8), 8)
+                b_re[to, :] = out[g * 8 : g * 8 + 8, :length]
+                b_im[to, :] = out[g * 8 : g * 8 + 8, length:]
+
+    def release(r):
+        for s in range(groups - 1):
+            send_all(r, s).wait_send()
+        keep(r).wait()
+
+    def forward(r, b_re, b_im, next_re, next_im):
+        q = lax.rem(r, 2)
 
         @pl.when(r + 1 < rotations)
         def _():
-            relay(r + 1)
+            finish(r + 1)
+
+        z_stage(jnp.minimum(r + 1, rotations - 1))
 
         @pl.when(r + 2 < rotations)
         def _():
-            begin(r + 2)
-
-        def lane_group(j, carry):
-            at = pl.ds(pl.multiple_of(j * 128, 128), 128)
-            upper, lower = split(jnp.concatenate([a_buf[0:rows, at], a_buf[rows : 2 * rows, at]], axis=1))
-            both = jnp.concatenate([upper, lower, upper], axis=1)
-            per = 128 // box
-            for i in range(per):
-                out = mul(both, wy_ref[i])
-                for g in range(rows // 8):
-                    to = pl.ds(pl.multiple_of((g * box + j * per + i) * 8, 8), 8)
-                    b_re[to, :] = out[g * 8 : g * 8 + 8, :length]
-                    b_im[to, :] = out[g * 8 : g * 8 + 8, length:]
-            return carry
-
-        lax.fori_loop(0, box * box // 128, lane_group, 0)
-
-        @pl.when(r == 0)
+            relay(r + 2)
+
+        @pl.when(r + 3 < rotations)
         def _():
-            rec_copy.wait()
+            begin(r + 3)
+
+        @pl.when(r >= 2)
+        def _():
+            release(r - 2)
 
         def x_stage(k, spec):
             for p in range(pairs):
@@ -171,7 +208,7 @@
                 def pick(ref):
                     parts = []
                     for c in pair:
-                        row = k * channels + c
+                        row = k * middle + c if c < middle else tops[0] + k * (channels - middle) + c - middle
                         parts.append(ref[pl.ds(row // 8 * (box * 8) + lax.rem(row, 8), box, stride=8), :])
                     return split(jnp.concatenate(parts, axis=1))
                 re_hi, re_lo = pick(b_re)
@@ -187,8 +224,8 @@
                     at = slice((c % 2) * length, (c % 2 + 1) * length)
                     s_re = spec[c // 2, low, at]
                     s_im = spec[c // 2, high, at]
-                    r_re = rec[0, c, k, low].astype(F32)
-                    r_im = rec[1, c, k, low].astype(F32)
+                    r_re = rec[0, c, k, low]
+                    r_im = rec[1, c, k, low]
                     q_re = r_re * s_re + r_im * s_im
                     q_im = r_im * s_re - r_re * s_im
                     p_re = q_re if p_re is None else p_re + q_re
@@ -205,16 +242,20 @@
             most = jnp.max(jnp.abs(field), axis=1, keepdims=True)
             code = jnp.ceil(LEVELS * jnp.log2(jnp.maximum(most, 1e-30))) + 1.0
             factor = TOP * jnp.exp2(code * (-1.0 / LEVELS))
-            qbuf[r, k] = jnp.round(field * factor).astype(jnp.int32).reshape(groups, xs, 2 * length).astype(jnp.int16)
+            qbuf[q, k] = jnp.round(field * factor).astype(jnp.int32).reshape(groups, xs, 2 * length).astype(jnp.int16)
             expo[...] = jnp.where(lanes == k, code, expo[...])
 
         def send(k):
             for s in range(groups - 1):
                 send_plane(r, k, s).start()
 
+        each = -(-lane_groups // (planes // 2))
+
         def two(m, carry):
             k = 2 * m
             x_stage(k - 1, spec_b)
+            for g in range(each):
+                lane_group(jnp.minimum((m - 1) * each + g, lane_groups - 1), next_re, next_im)
             product(k - 2, spec_a, square_a)
             close(jnp.maximum(k - 3, 0), square_b)
             x_stage(k, spec_a)
@@ -237,21 +278,49 @@
         send(planes - 1)
         codes = expo[...].astype(jnp.int32)
         codes = jnp.concatenate([codes, codes], axis=1)
-        qbuf[r, planes] = codes.reshape(groups, xs, 2 * length).astype(jnp.int16)
+        qbuf[q, planes] = codes.reshape(groups, xs, 2 * length).astype(jnp.int16)
         send(planes)
         keep(r).start()
 
-    begin(0)
+    for r in range(min(3, rotations)):
+        begin(r)
+
+    def widen(k, carry):
+        @pl.when(k + 1 < planes)
+        def _():
+            fetch(k + 1).start()
+
+        fetch(k).wait()
+        for part in range(2):
+            for c in range(channels):
+                rec[part, c, k] = stage[lax.rem(k, 2), part, c].astype(F32)
+        return carry
+
+    lax.fori_loop(0, planes, widen, 0)
+    for copy in table_copies:
+        copy.wait()
+    relay(0)
+    finish(0)
+    z_stage(0)
     if rotations > 1:
-        begin(1)
-    tz_copy.wait()
-    relay(0)
-
-    def rotation(r, carry):
-        forward(r)
+        relay(1)
+
+    def first(j, carry):
+        lane_group(j, even_re, even_im)
         return carry
 
-    lax.fori_loop(0, rotations, rotation, 0)
+    lax.fori_loop(0, lane_groups, first, 0)
+
+    def rotation_pair(p, carry):
+        forward(2 * p, even_re, even_im, odd_re, odd_im)
+        forward(2 * p + 1, odd_re, odd_im, even_re, even_im)
+        return carry
+
+    lax.fori_loop(0, rotations // 2, rotation_pair, 0)
+    if rotations % 2:
+        forward(rotations - 1, even_re, even_im, odd_re, odd_im)
+    for r in range(max(rotations - 2, 0), rotations):
+        release(r)
 
     def drain(r, carry):
         for k in range(len(peers)):
@@ -259,9 +328,7 @@
         for k in range(len(far)):
             relay_copy(r, k).wait_send()
         for s in range(groups - 1):
-            send_all(r, s).wait_send()
             send_all(r, s).wait_recv()
-        keep(r).wait()
         return carry
 
     lax.fori_loop(0, rotations, drain, 0)
@@ -294,6 +361,36 @@
             out_ref[0, i + t] = plane.T
 
 
+def best_kernel(groups, rotations, lows_ref, out_ref, held, send_sem, recv_sem):
+    me = lax.axis_index("fft")
+    others = [lax.rem(me + s, groups) for s in range(1, groups)]
+    barrier = pltpu.get_barrier_semaphore()
+    for peer in others:
+        pl.semaphore_signal(barrier, inc=1, device_id={"fft": peer}, device_id_type=pl.DeviceIdType.MESH)
+    held[me] = jnp.min(lows_ref[...], axis=(1, 2))
+    pl.semaphore_wait(barrier, groups - 1)
+
+    def share(s):
+        return pltpu.make_async_remote_copy(
+            src_ref=held.at[me], dst_ref=held.at[me], send_sem=send_sem.at[s], recv_sem=recv_sem.at[me],
+            device_id={"fft": others[s]}, device_id_type=pl.DeviceIdType.MESH)
+
+    def arrival(s):
+        return pltpu.make_async_remote_copy(
+            src_ref=held.at[me], dst_ref=held.at[others[s]], send_sem=send_sem.at[s], recv_sem=recv_sem.at[others[s]],
+            device_id={"fft": others[s]}, device_id_type=pl.DeviceIdType.MESH)
+
+    for s in range(groups - 1):
+        share(s).start()
+    for s in range(groups - 1):
+        arrival(s).wait_recv()
+        share(s).wait_send()
+    low = jnp.min(jnp.min(held[...], axis=0), axis=1, keepdims=True)
+    lane = lax.broadcasted_iota(jnp.int32, (rotations, 128), 1)
+    row = lax.broadcasted_iota(jnp.int32, (rotations, 128), 0)
+    out_ref[...] = jnp.sum(jnp.where(lane == row, low, 0.0), axis=0, keepdims=True)[:, :rotations]
+
+
 def shards(receptor, ligand_grids, rot_index):
     groups = lax.axis_size("fft")
     channels, slab, length = receptor.shape[1], receptor.shape[2], receptor.shape[3]
@@ -303,31 +400,39 @@
     rotations = rot_index.shape[0]
     xs = length // groups
     planes = slab // 2 + 1
-    block = up(channels * depth, 16)
-    rows = up(planes * channels, 16)
+    middle = (channels + 1) // 2
+    cuts = tuple((start, stop, up((stop - start) * depth, 16)) for start, stop in ((0, middle), (middle, channels)))
+    block = cuts[0][2] + cuts[1][2]
+    top = up(planes * middle, 8)
+    rows = up(top + planes * (channels - middle), 16)
+    tops = (top, rows - top)
     freq = np.arange(length)
 
-    t_z = np.zeros((groups, 2, rows, groups, block))
-    for d in range(groups):
-        cz, sz = trig(d * slab + np.arange(planes), np.arange(box), length)
-        for c in range(channels):
-            at = np.arange(planes) * channels + c
-            for s in range(groups):
-                span = slice(c * depth, (c + 1) * depth)
-                cut = slice(s * depth, (s + 1) * depth)
-                t_z[d, 0, at, s, span] = cz[:, cut]
-                t_z[d, 1, at, s, span] = -sz[:, cut]
-    t_z = t_z.reshape(groups, 2 * rows, groups * block)
-    t_z = jnp.asarray(np.stack(halves(t_z), axis=1))
+    t_z = []
+    for (start, stop, size), top in zip(cuts, tops):
+        table = np.zeros((groups, 2, top, groups, size))
+        for d in range(groups):
+            cz, sz = trig(d * slab + np.arange(planes), np.arange(box), length)
+            for c in range(stop - start):
+                at = np.arange(planes) * (stop - start) + c
+                for s in range(groups):
+                    span = slice(c * depth, (c + 1) * depth)
+                    cut = slice(s * depth, (s + 1) * depth)
+                    table[d, 0, at, s, span] = cz[:, cut]
+                    table[d, 1, at, s, span] = -sz[:, cut]
+        table = table.reshape(groups, 2 * top, groups * size)
+        t_z.append(jnp.asarray(np.stack(halves(table), axis=1)))
 
     cy, sy = trig(np.arange(box), freq, length)
     per = 128 // box
-    w_y = np.zeros((per, 256, 2 * length))
+    hi, lo = halves(np.concatenate([cy, -sy], axis=1)), halves(np.concatenate([sy, cy], axis=1))
+    w_y = np.zeros((per, 512, 2 * length), ml_dtypes.bfloat16)
     for i in range(per):
-        w_y[i, i * box : (i + 1) * box] = np.concatenate([cy, -sy], axis=1)
-        w_y[i, 128 + i * box : 128 + (i + 1) * box] = np.concatenate([sy, cy], axis=1)
-    hi, lo = halves(w_y)
-    w_y = jnp.asarray(np.concatenate([hi, hi, lo], axis=1))
+        for part, (upper, lower) in enumerate((hi, lo)):
+            for spot in (i * box, (i * box + 64) % 128):
+                w_y[i, part * 128 + spot : part * 128 + spot + box] = upper
+            w_y[i, 256 + part * 128 + i * box : 256 + part * 128 + (i + 1) * box] = lower
+    w_y = jnp.asarray(w_y)
 
     t_x = np.block([[cy.T, sy.T], [-sy.T, cy.T]])
     hi, lo = halves(t_x)
@@ -356,7 +461,7 @@
     t_w = jnp.asarray(np.concatenate([hi, lo, hi], axis=0))
 
     own = pl.pallas_call(
-        functools.partial(pick_kernel, channels, block),
+        functools.partial(pick_kernel, cuts),
         grid_spec=pltpu.PrefetchScalarGridSpec(
             num_scalar_prefetch=1,
             grid=(rotations,),
@@ -369,15 +474,19 @@
     any_space = pl.BlockSpec(memory_space=pl.ANY)
     vmem = pl.BlockSpec(memory_space=pltpu.VMEM)
     sent = pl.pallas_call(
-        functools.partial(main_kernel, channels, planes, box, groups, rotations, length, block, rows),
-        in_specs=[any_space, any_space, any_space, vmem, vmem, vmem],
+        functools.partial(main_kernel, channels, planes, box, groups, rotations, length, cuts, tops),
+        in_specs=[any_space, any_space, any_space, any_space, vmem, vmem, vmem],
         out_specs=any_space,
         out_shape=jax.ShapeDtypeStruct((rotations, groups, planes + 1, xs, 2 * length), jnp.int16),
         scratch_shapes=[
-            pltpu.VMEM((2, channels, planes, length, length), BF),
+            pltpu.VMEM((2, channels, planes, length, length), F32),
+            pltpu.VMEM((2, 2, channels, length, length), BF),
             pltpu.VMEM((rotations, groups * block, cells), BF),
-            pltpu.VMEM((2, 2 * rows, groups * block), BF),
+            pltpu.VMEM(t_z[0].shape[1:], BF),
+            pltpu.VMEM(t_z[1].shape[1:], BF),
             pltpu.VMEM((2 * rows, cells), F32),
+            pltpu.VMEM((rows * box, length), F32),
+            pltpu.VMEM((rows * box, length), F32),
             pltpu.VMEM((rows * box, length), F32),
             pltpu.VMEM((rows * box, length), F32),
             pltpu.VMEM((-(-channels // 2), 2 * length, 2 * length), F32),
@@ -385,8 +494,8 @@
             pltpu.VMEM((2, 2 * length, 2 * length), BF),
             pltpu.VMEM((2, 2 * length, 2 * length), BF),
             pltpu.VMEM((length, length), F32),
-            pltpu.VMEM((rotations, planes + 1, groups, xs, 2 * length), jnp.int16),
-            pltpu.SemaphoreType.DMA((2,)),
+            pltpu.VMEM((2, planes + 1, groups, xs, 2 * length), jnp.int16),
+            pltpu.SemaphoreType.DMA((4,)),
             pltpu.SemaphoreType.DMA((rotations,)),
             pltpu.SemaphoreType.DMA((rotations, groups)),
             pltpu.SemaphoreType.DMA((rotations, groups)),
@@ -395,9 +504,9 @@
             pltpu.SemaphoreType.DMA((rotations,)),
         ],
         compiler_params=pltpu.CompilerParams(
-            collective_id=0, has_side_effects=True, vmem_limit_bytes=56 * 2**20),
+            collective_id=0, has_side_effects=True, vmem_limit_bytes=60 * 2**20),
         cost_estimate=pl.CostEstimate(flops=rotations * 6 * 10**9, bytes_accessed=30_000_000, transcendentals=0),
-    )(receptor, own, t_z, w_y, t_x, t_i)
+    )(receptor, own, *t_z, w_y, t_x, t_i)
 
     width = min(16, xs)
     scores, lows = pl.pallas_call(
@@ -417,11 +526,22 @@
             jax.ShapeDtypeStruct((rotations, xs // width, width, length), F32),
         ],
         scratch_shapes=[pltpu.VMEM((terms * width, length), F32)] * 2,
-        compiler_params=pltpu.CompilerParams(vmem_limit_bytes=32 * 2**20),
+        compiler_params=pltpu.CompilerParams(vmem_limit_bytes=60 * 2**20),
         cost_estimate=pl.CostEstimate(flops=rotations * 10**9, bytes_accessed=20_000_000, transcendentals=0),
     )(sent, t_w, t_b)
-    best = lax.pmin(jnp.min(lows, axis=(1, 2, 3)), "fft")
-    return scores, best
+    best = pl.pallas_call(
+        functools.partial(best_kernel, groups, rotations),
+        in_specs=[vmem],
+        out_specs=vmem,
+        out_shape=jax.ShapeDtypeStruct((1, rotations), F32),
+        scratch_shapes=[
+            pltpu.VMEM((groups, rotations, length), F32),
+            pltpu.SemaphoreType.DMA((groups,)),
+            pltpu.SemaphoreType.DMA((groups,)),
+        ],
+        compiler_params=pltpu.CompilerParams(collective_id=1, has_side_effects=True),
+    )(lows)
+    return scores, best.reshape(rotations)
 
 
 def solution(mesh):

time: 149 us -> 145 us (0.973)
  blocking collectives: 6.25 us -> 0 us
  Pallas kernels: 138 us -> 142 us
  local copies, waits for them, and re-layouts: 3.01 us -> 1.11 us
    pmin x1 -> x0, blocking collectives: 6.25 us -> none  [shards(): best = lax.pmin(jnp.min(lows, axis=(1, 2, 3)), 'fft')]
    pallas_call x1 -> x2, Pallas kernels: 5.03 us -> 10.2 us  [the longest x1 5.15 us: shards(): pl.pallas_call(functools.partial(best_kernel, groups, rotations), in_spec...]
    pallas_call x1, Pallas kernels: 114 us -> 112 us  [shards(): pl.pallas_call(functools.partial(main_kernel, channels, planes, box, grou...]
    unnamed x6 -> x1, local copies, waits for them, and re-layouts: 3.01 us -> 1.11 us
where the time goes in v3:
time: 145 us; the launch traced here: 144 us
  Pallas kernels  142 us (98%)
    pallas_call x1, Pallas kernels, shards(): pl.pallas_call(functools.partial(main_kernel, channels, planes, box, grou...  112 us
    pallas_call x1, Pallas kernels, shards(): pl.pallas_call(functools.partial(final_kernel, groups, planes, length, wi...  20 us
    pallas_call x1, Pallas kernels, shards(): pl.pallas_call(functools.partial(best_kernel, groups, rotations), in_spec...  5.15 us
    pallas_call x1, Pallas kernels, shards(): pl.pallas_call(functools.partial(pick_kernel, cuts), grid_spec=pltpu.Pref...  5.03 us

profile of v3, /device:TPU:0, one launch (start us, length us, event | category | flops | bytes accessed | tf_op | source)
XLA Modules:
  0.0 143.9 jit_solution(982635389005121806)
XLA Ops:
  0.6 5.0 %shard_map.113.own_hbm = bf16[6,96,1024]{2,1,0:T(8,128)(2,1)} custom-call(s32[6]{0:T(128)} %index_ref.1, bf16[32,11,8,1024]{3,2,1,0:T(8,128)(2,1)} %in_ref.1), custom_call_target="tpu_custom_call" | custom-call | tf_op jit(solution)/shard_map/pallas_call | solution.py:463
  5.7 111.9 %shard_map.114.blocks_ref = s16[6,4,18,32,256]{4,3,2,1,0:T(8,128)(2,1)} custom-call(bf16[2,11,32,128,128]{4,3,2,1,0:T(8,128)(2,1)} %rec_hbm.1, bf16[6,96,1024]{2,1,0:T(8,128)(2,1)} %shard_map.113.own_hbm, bf16[4,2,208,192]{3,2,1,0:T(8,128)(2,1)} %constant.14.clone.tza_hbm, bf16[4,2,176,192]{3,2,1,0:T(8,128)(2,1)} %constant.15.clone.tzb_hbm, ...), custom_call_target="tpu_custom_call" | custom-call | flops 35999997952 | bytes 30000000 | tf_op jit(solution)/shard_map/pallas_call | solution.py:476
  117.6 20.0 %shard_map.115 = (f32[6,32,128,128]{3,2,1,0:T(8,128)}, f32[6,2,16,128]{3,2,1,0:T(8,128)}) custom-call(s16[6,4,18,32,256]{4,3,2,1,0:T(8,128)(2,1)} %shard_map.114.blocks_ref, bf16[768,256]{1,0:T(8,128)(2,1)} %constant.20.clone.ty_ref, bf16[128,480]{1,0:T(8,128)(2,1)} %constant.19.clone.tz_ref), custom_call_target="tpu_custom_call" | custom-call | flops 6000000000 | bytes 20000000 | tf_op jit(solution)/shard_map/pallas_call | solution.py:512
  137.6 5.2 %shard_map.116 = f32[1,6]{1,0:T(1,128)} custom-call(f32[6,2,16,128]{3,2,1,0:T(8,128)} %get-tuple-element.5.lows_ref), custom_call_target="tpu_custom_call" | custom-call | tf_op jit(solution)/shard_map/pallas_call | solution.py:532
  142.8 1.1 copy.13

commit v4 on v3

--- a/solution.py
+++ b/solution.py
@@ -55,10 +55,10 @@
 
 
 def main_kernel(
-    channels, planes, box, groups, rotations, length, cuts, tops,
-    rec_hbm, own_hbm, tza_hbm, tzb_hbm, wy_ref, tx_ref, ti_ref, recv_hbm,
-    rec, stage, lbuf, tza, tzb, a_buf, even_re, even_im, odd_re, odd_im, spec_a, spec_b, square_a, square_b, expo, qbuf,
-    load_sem, own_sem, gsend, grecv, xsend, xrecv, self_sem,
+    channels, planes, box, groups, rotations, length, cuts, tops, width, terms,
+    rec_hbm, own_hbm, tza_hbm, tzb_hbm, wy_ref, tx_ref, ti_ref, ty_ref, tb_ref, recv_hbm, early_hbm, low_ref,
+    rec, stage, lbuf, tza, tzb, a_buf, even_re, even_im, odd_re, odd_im, spec_a, spec_b, square_a, square_b, expo, qbuf, blocks, ready, h_re, h_im,
+    load_sem, own_sem, gsend, grecv, xsend, xrecv, self_sem, in_sem, out_sem,
 ):
     me = lax.axis_index("fft")
     block = cuts[0][2] + cuts[1][2]
@@ -311,9 +311,35 @@
 
     lax.fori_loop(0, lane_groups, first, 0)
 
+    parts = xs // width
+
+    def load_block(f, h):
+        return pltpu.make_async_copy(recv_hbm.at[f, :, :, pl.ds(h * width, width)], blocks.at[h], in_sem.at[h])
+
+    def store_block(f, h):
+        return pltpu.make_async_copy(ready.at[h], early_hbm.at[f, pl.ds(h * width, width)], out_sem.at[h])
+
+    def end(f, carry):
+        for s in range(groups - 1):
+            send_all(f, s).wait_recv()
+        for h in range(parts):
+            load_block(f, h).start()
+        for h in range(parts):
+            @pl.when(f > 0)
+            def _():
+                store_block(f - 1, h).wait()
+
+            load_block(f, h).wait()
+            end_block(
+                groups, planes, length, width, terms, lambda s, k: blocks[h, s, k], ty_ref, tb_ref,
+                ready.at[h], low_ref.at[f, h], h_re, h_im)
+            store_block(f, h).start()
+        return carry
+
     def rotation_pair(p, carry):
         forward(2 * p, even_re, even_im, odd_re, odd_im)
         forward(2 * p + 1, odd_re, odd_im, even_re, even_im)
+        lax.fori_loop(jnp.maximum(2 * p - 2, 0), 2 * p, end, 0)
         return carry
 
     lax.fori_loop(0, rotations // 2, rotation_pair, 0)
@@ -321,24 +347,30 @@
         forward(rotations - 1, even_re, even_im, odd_re, odd_im)
     for r in range(max(rotations - 2, 0), rotations):
         release(r)
+    early = 2 * (rotations // 2) - 2
+    for h in range(parts):
+        store_block(early - 1, h).wait()
 
     def drain(r, carry):
         for k in range(len(peers)):
             own_copy(r, k).wait_send()
         for k in range(len(far)):
             relay_copy(r, k).wait_send()
-        for s in range(groups - 1):
-            send_all(r, s).wait_recv()
+        @pl.when(r >= early)
+        def _():
+            for s in range(groups - 1):
+                send_all(r, s).wait_recv()
+
         return carry
 
     lax.fori_loop(0, rotations, drain, 0)
 
 
-def final_kernel(groups, planes, length, width, terms, blocks_ref, ty_ref, tz_ref, out_ref, low_ref, h_re, h_im):
+def end_block(groups, planes, length, width, terms, read, ty_ref, tz_ref, out_ref, low_ref, h_re, h_im):
     for s in range(groups):
-        code = blocks_ref[0, s, planes].astype(jnp.int32).astype(F32)[:, :length]
+        code = read(s, planes).astype(jnp.int32).astype(F32)[:, :length]
         scale = jnp.exp2(code * (1.0 / LEVELS)) * (1.0 / TOP)
-        parts = [blocks_ref[0, s, k].astype(jnp.int32).astype(F32) * scale[:, k : k + 1] for k in range(planes)]
+        parts = [read(s, k).astype(jnp.int32).astype(F32) * scale[:, k : k + 1] for k in range(planes)]
         upper, lower = split(jnp.concatenate(parts, axis=0))
         lines = mul(jnp.concatenate([upper, upper, lower], axis=1), ty_ref[...])
         at = pl.ds(s * planes * width, planes * width)
@@ -357,17 +389,62 @@
         field = mul(tz_ref[...], right)
         for t in range(2):
             plane = field[:, t * length : (t + 1) * length]
-            low_ref[0, 0, i + t : i + t + 1, :] = jnp.min(plane, axis=0, keepdims=True)
-            out_ref[0, i + t] = plane.T
-
-
-def best_kernel(groups, rotations, lows_ref, out_ref, held, send_sem, recv_sem):
+            low_ref[i + t : i + t + 1, :] = jnp.min(plane, axis=0, keepdims=True)
+            out_ref[i + t] = plane.T
+
+
+def final_kernel(
+    groups, planes, length, width, terms, early, parts, steps,
+    blocks_ref, early_hbm, ty_ref, tz_ref, out_hbm, low_ref, ready, h_re, h_im, hold, copy_sem, out_sem,
+):
+    step = pl.program_id(0) * parts + pl.program_id(1)
+
+    def store_block(t):
+        at = pl.ds(pl.multiple_of(lax.rem(t, parts) * width, width), width)
+        return pltpu.make_async_copy(ready.at[lax.rem(t, 2)], out_hbm.at[early + t // parts, at], out_sem.at[lax.rem(t, 2)])
+
+    def bring(r):
+        return pltpu.make_async_copy(early_hbm.at[r], hold.at[r], copy_sem.at[0, r])
+
+    def hand(r):
+        return pltpu.make_async_copy(hold.at[r], out_hbm.at[r], copy_sem.at[1, r])
+
+    @pl.when(step == 0)
+    def _():
+        for r in range(early):
+            bring(r).start()
+
+    @pl.when(step >= 2)
+    def _():
+        store_block(step - 2).wait()
+
+    end_block(
+        groups, planes, length, width, terms, lambda s, k: blocks_ref[0, s, k], ty_ref, tz_ref,
+        ready.at[lax.rem(step, 2)], low_ref.at[0, 0], h_re, h_im)
+    store_block(step).start()
+    for r in range(early):
+        @pl.when(step == r * steps // early)
+        def _():
+            bring(r).wait()
+            hand(r).start()
+
+    @pl.when(step == steps - 1)
+    def _():
+        if steps > 1:
+            store_block(step - 1).wait()
+        store_block(step).wait()
+        for r in range(early):
+            hand(r).wait()
+
+
+def best_kernel(groups, rotations, early, first_ref, last_ref, out_ref, held, send_sem, recv_sem):
     me = lax.axis_index("fft")
     others = [lax.rem(me + s, groups) for s in range(1, groups)]
     barrier = pltpu.get_barrier_semaphore()
     for peer in others:
         pl.semaphore_signal(barrier, inc=1, device_id={"fft": peer}, device_id_type=pl.DeviceIdType.MESH)
-    held[me] = jnp.min(lows_ref[...], axis=(1, 2))
+    held[me, 0:early] = jnp.min(first_ref[...], axis=(1, 2))
+    held[me, early:rotations] = jnp.min(last_ref[...], axis=(1, 2))
     pl.semaphore_wait(barrier, groups - 1)
 
     def share(s):
@@ -473,11 +550,19 @@
 
     any_space = pl.BlockSpec(memory_space=pl.ANY)
     vmem = pl.BlockSpec(memory_space=pltpu.VMEM)
-    sent = pl.pallas_call(
-        functools.partial(main_kernel, channels, planes, box, groups, rotations, length, cuts, tops),
-        in_specs=[any_space, any_space, any_space, any_space, vmem, vmem, vmem],
-        out_specs=any_space,
-        out_shape=jax.ShapeDtypeStruct((rotations, groups, planes + 1, xs, 2 * length), jnp.int16),
+    width = min(16, xs)
+    parts = xs // width
+    early = 2 * (rotations // 2) - 2
+    late = rotations - early
+    sent, early_scores, early_lows = pl.pallas_call(
+        functools.partial(main_kernel, channels, planes, box, groups, rotations, length, cuts, tops, width, terms),
+        in_specs=[any_space] * 4 + [vmem] * 5,
+        out_specs=[any_space, any_space, vmem],
+        out_shape=[
+            jax.ShapeDtypeStruct((rotations, groups, planes + 1, xs, 2 * length), jnp.int16),
+            jax.ShapeDtypeStruct((early, xs, length, length), F32),
+            jax.ShapeDtypeStruct((early, parts, width, length), F32),
+        ],
         scratch_shapes=[
             pltpu.VMEM((2, channels, planes, length, length), F32),
             pltpu.VMEM((2, 2, channels, length, length), BF),
@@ -495,6 +580,10 @@
             pltpu.VMEM((2, 2 * length, 2 * length), BF),
             pltpu.VMEM((length, length), F32),
             pltpu.VMEM((2, planes + 1, groups, xs, 2 * length), jnp.int16),
+            pltpu.VMEM((parts, groups, planes + 1, width, 2 * length), jnp.int16),
+            pltpu.VMEM((parts, width, length, length), F32),
+            pltpu.VMEM((terms * width, length), F32),
+            pltpu.VMEM((terms * width, length), F32),
             pltpu.SemaphoreType.DMA((4,)),
             pltpu.SemaphoreType.DMA((rotations,)),
             pltpu.SemaphoreType.DMA((rotations, groups)),
@@ -502,36 +591,42 @@
             pltpu.SemaphoreType.DMA((rotations, groups)),
             pltpu.SemaphoreType.DMA((rotations, groups)),
             pltpu.SemaphoreType.DMA((rotations,)),
+            pltpu.SemaphoreType.DMA((parts,)),
+            pltpu.SemaphoreType.DMA((parts,)),
         ],
         compiler_params=pltpu.CompilerParams(
             collective_id=0, has_side_effects=True, vmem_limit_bytes=60 * 2**20),
         cost_estimate=pl.CostEstimate(flops=rotations * 6 * 10**9, bytes_accessed=30_000_000, transcendentals=0),
-    )(receptor, own, *t_z, w_y, t_x, t_i)
-
-    width = min(16, xs)
-    scores, lows = pl.pallas_call(
-        functools.partial(final_kernel, groups, planes, length, width, terms),
-        grid=(rotations, xs // width),
+    )(receptor, own, *t_z, w_y, t_x, t_i, t_w, t_b)
+
+    scores, late_lows = pl.pallas_call(
+        functools.partial(final_kernel, groups, planes, length, width, terms, early, parts, late * parts),
+        grid=(late, parts),
         in_specs=[
-            pl.BlockSpec((1, groups, planes + 1, width, 2 * length), lambda r, x: (r, 0, 0, x, 0)),
+            pl.BlockSpec((1, groups, planes + 1, width, 2 * length), lambda r, x: (early + r, 0, 0, x, 0)),
+            any_space,
             pl.BlockSpec(t_w.shape, lambda r, x: (0, 0)),
             pl.BlockSpec(t_b.shape, lambda r, x: (0, 0)),
         ],
-        out_specs=[
-            pl.BlockSpec((1, width, length, length), lambda r, x: (r, x, 0, 0)),
-            pl.BlockSpec((1, 1, width, length), lambda r, x: (r, x, 0, 0)),
-        ],
+        out_specs=[any_space, pl.BlockSpec((1, 1, width, length), lambda r, x: (r, x, 0, 0))],
         out_shape=[
             jax.ShapeDtypeStruct((rotations, xs, length, length), F32),
-            jax.ShapeDtypeStruct((rotations, xs // width, width, length), F32),
+            jax.ShapeDtypeStruct((late, parts, width, length), F32),
         ],
-        scratch_shapes=[pltpu.VMEM((terms * width, length), F32)] * 2,
+        scratch_shapes=[
+            pltpu.VMEM((2, width, length, length), F32),
+            pltpu.VMEM((terms * width, length), F32),
+            pltpu.VMEM((terms * width, length), F32),
+            pltpu.VMEM((early, xs, length, length), F32),
+            pltpu.SemaphoreType.DMA((2, early)),
+            pltpu.SemaphoreType.DMA((2,)),
+        ],
         compiler_params=pltpu.CompilerParams(vmem_limit_bytes=60 * 2**20),
-        cost_estimate=pl.CostEstimate(flops=rotations * 10**9, bytes_accessed=20_000_000, transcendentals=0),
-    )(sent, t_w, t_b)
+        cost_estimate=pl.CostEstimate(flops=late * 10**9, bytes_accessed=20_000_000, transcendentals=0),
+    )(sent, early_scores, t_w, t_b)
     best = pl.pallas_call(
-        functools.partial(best_kernel, groups, rotations),
-        in_specs=[vmem],
+        functools.partial(best_kernel, groups, rotations, early),
+        in_specs=[vmem, vmem],
         out_specs=vmem,
         out_shape=jax.ShapeDtypeStruct((1, rotations), F32),
         scratch_shapes=[
@@ -540,7 +635,7 @@
             pltpu.SemaphoreType.DMA((groups,)),
         ],
         compiler_params=pltpu.CompilerParams(collective_id=1, has_side_effects=True),
-    )(lows)
+    )(early_lows, late_lows)
     return scores, best.reshape(rotations)
 
 

time: 145 us -> 140 us (0.966)
  Pallas kernels: 142 us -> 138 us
    pallas_call x1, Pallas kernels: 20 us -> 12.5 us  [shards(): pl.pallas_call(functools.partial(final_kernel, groups, planes, length, wi...]
    pallas_call x1, Pallas kernels: 112 us -> 115 us  [shards(): pl.pallas_call(functools.partial(main_kernel, channels, planes, box, grou...]
where the time goes in v4:
time: 140 us
  Pallas kernels  138 us (99%)
    pallas_call x1, Pallas kernels, shards(): pl.pallas_call(functools.partial(main_kernel, channels, planes, box, grou...  115 us
    pallas_call x1, Pallas kernels, shards(): pl.pallas_call(functools.partial(final_kernel, groups, planes, length, wi...  12.5 us
    pallas_call x1, Pallas kernels, shards(): pl.pallas_call(functools.partial(best_kernel, groups, rotations, early),...  5.14 us
    pallas_call x1, Pallas kernels, shards(): pl.pallas_call(functools.partial(pick_kernel, cuts), grid_spec=pltpu.Pref...  5.03 us

profile of v4, /device:TPU:0, one launch (start us, length us, event | category | flops | bytes accessed | tf_op | source)
XLA Modules:
  0.0 139.5 jit_solution(14109856769346681464)
XLA Ops:
  0.6 5.0 %shard_map.113.own_hbm = bf16[6,96,1024]{2,1,0:T(8,128)(2,1)} custom-call(s32[6]{0:T(128)} %index_ref.1, bf16[32,11,8,1024]{3,2,1,0:T(8,128)(2,1)} %in_ref.1), custom_call_target="tpu_custom_call" | custom-call | tf_op jit(solution)/shard_map/pallas_call | solution.py:540
  5.7 115.1 %shard_map.114 = (s16[6,4,18,32,256]{4,3,2,1,0:T(8,128)(2,1)}, f32[4,32,128,128]{3,2,1,0:T(8,128)}, f32[4,2,16,128]{3,2,1,0:T(8,128)}) custom-call(bf16[2,11,32,128,128]{4,3,2,1,0:T(8,128)(2,1)} %rec_hbm.1, bf16[6,96,1024]{2,1,0:T(8,128)(2,1)} %shard_map.113.own_hbm, bf16[4,2,208,192]{3,2,1,0:T(8,128)(2,1)} %constant.14.clone.tza_hbm, ...), custom_call_target="tpu_custom_call" | custom-call | flops 35999997952 | bytes 30000000 | tf_op jit(solution)/shard_map/pallas_call | solution.py:557
  120.8 12.5 %shard_map.115 = (f32[6,32,128,128]{3,2,1,0:T(8,128)}, f32[2,2,16,128]{3,2,1,0:T(8,128)}) custom-call(s16[6,4,18,32,256]{4,3,2,1,0:T(8,128)(2,1)} %get-tuple-element.7.blocks_ref, f32[4,32,128,128]{3,2,1,0:T(8,128)} %get-tuple-element.8.early_hbm, bf16[768,256]{1,0:T(8,128)(2,1)} %constant.20.clone.ty_ref, bf16[128,480]{1,0:T(8,128)(2,1)} %constant.19.clone.tb_ref.tz_ref), custom_call_target="tpu_custom_call" | custom-call | flops 2000000000 | bytes 20000000 | tf_op jit(solution)/shard_map/pallas_call | solution.py:602
  133.3 5.1 %shard_map.116 = f32[1,6]{1,0:T(1,128)} custom-call(f32[4,2,16,128]{3,2,1,0:T(8,128)} %get-tuple-element.10.first_ref, f32[2,2,16,128]{3,2,1,0:T(8,128)} %get-tuple-element.11.last_ref), custom_call_target="tpu_custom_call" | custom-call | tf_op jit(solution)/shard_map/pallas_call | solution.py:627
  138.4 1.1 copy.13

commit v5 on v4

--- a/solution.py
+++ b/solution.py
@@ -44,14 +44,22 @@
     return -(-value // step) * step
 
 
-def pick_kernel(cuts, index_ref, in_ref, out_ref):
-    depth, cells = in_ref.shape[2], in_ref.shape[3]
-    parts = []
-    for start, stop, size in cuts:
-        parts += [in_ref[0, c].astype(F32) for c in range(start, stop)]
-        if size > (stop - start) * depth:
-            parts.append(jnp.zeros((size - (stop - start) * depth, cells), F32))
-    out_ref[0] = jnp.concatenate(parts, axis=0).astype(BF)
+def pick_kernel(cuts, index_ref, table_hbm, out_ref, held, sems):
+    rotations, depth, cells = held.shape[0], held.shape[2], held.shape[3]
+
+    def fetch(r):
+        return pltpu.make_async_copy(table_hbm.at[index_ref[r]], held.at[r], sems.at[r])
+
+    for r in range(rotations):
+        fetch(r).start()
+    for r in range(rotations):
+        fetch(r).wait()
+        parts = []
+        for start, stop, size in cuts:
+            parts += [held[r, c].astype(F32) for c in range(start, stop)]
+            if size > (stop - start) * depth:
+                parts.append(jnp.zeros((size - (stop - start) * depth, cells), F32))
+        out_ref[r] = jnp.concatenate(parts, axis=0).astype(BF)
 
 
 def main_kernel(
@@ -414,6 +422,12 @@
         for r in range(early):
             bring(r).start()
 
+    for r in range(early):
+        @pl.when(step == min(r + 1, steps - 1))
+        def _():
+            bring(r).wait()
+            hand(r).start()
+
     @pl.when(step >= 2)
     def _():
         store_block(step - 2).wait()
@@ -422,12 +436,6 @@
         groups, planes, length, width, terms, lambda s, k: blocks_ref[0, s, k], ty_ref, tz_ref,
         ready.at[lax.rem(step, 2)], low_ref.at[0, 0], h_re, h_im)
     store_block(step).start()
-    for r in range(early):
-        @pl.when(step == r * steps // early)
-        def _():
-            bring(r).wait()
-            hand(r).start()
-
     @pl.when(step == steps - 1)
     def _():
         if steps > 1:
@@ -537,19 +545,19 @@
     hi, lo = halves(np.block([[cf, sf], [-sf, cf]]) / float(length) ** 3)
     t_w = jnp.asarray(np.concatenate([hi, lo, hi], axis=0))
 
+    any_space = pl.BlockSpec(memory_space=pl.ANY)
+    vmem = pl.BlockSpec(memory_space=pltpu.VMEM)
     own = pl.pallas_call(
         functools.partial(pick_kernel, cuts),
-        grid_spec=pltpu.PrefetchScalarGridSpec(
-            num_scalar_prefetch=1,
-            grid=(rotations,),
-            in_specs=[pl.BlockSpec((1, channels, depth, cells), lambda r, index: (index[r], 0, 0, 0))],
-            out_specs=pl.BlockSpec((1, block, cells), lambda r, index: (r, 0, 0)),
-        ),
+        in_specs=[pl.BlockSpec(memory_space=pltpu.SMEM), any_space],
+        out_specs=vmem,
         out_shape=jax.ShapeDtypeStruct((rotations, block, cells), BF),
+        scratch_shapes=[
+            pltpu.VMEM((rotations, channels, depth, cells), BF),
+            pltpu.SemaphoreType.DMA((rotations,)),
+        ],
     )(rot_index, ligand_grids)
 
-    any_space = pl.BlockSpec(memory_space=pl.ANY)
-    vmem = pl.BlockSpec(memory_space=pltpu.VMEM)
     width = min(16, xs)
     parts = xs // width
     early = 2 * (rotations // 2) - 2

time: 140 us -> 137 us (0.979)
  Pallas kernels: 138 us -> 135 us
    pallas_call x1, Pallas kernels: 5.03 us -> 3.04 us  [shards(): pl.pallas_call(functools.partial(pick_kernel, cuts), in_specs=[pl.BlockSp...]
where the time goes in v5:
time: 137 us; the launch traced here: 136 us
  Pallas kernels  135 us (99%)
    pallas_call x1, Pallas kernels, shards(): pl.pallas_call(functools.partial(main_kernel, channels, planes, box, grou...  115 us
    pallas_call x1, Pallas kernels, shards(): pl.pallas_call(functools.partial(final_kernel, groups, planes, length, wi...  11.3 us
    pallas_call x1, Pallas kernels, shards(): pl.pallas_call(functools.partial(best_kernel, groups, rotations, early),...  5.14 us
    pallas_call x1, Pallas kernels, shards(): pl.pallas_call(functools.partial(pick_kernel, cuts), in_specs=[pl.BlockSp...  3.04 us

profile of v5, /device:TPU:0, one launch (start us, length us, event | category | flops | bytes accessed | tf_op | source)
XLA Modules:
  0.0 136.4 jit_solution(6633290425587158814)
XLA Ops:
  0.6 3.0 %shard_map.113.own_hbm = bf16[6,96,1024]{2,1,0:T(8,128)(2,1)} custom-call(s32[6]{0:T(128)} %index_ref.1, bf16[32,11,8,1024]{3,2,1,0:T(8,128)(2,1)} %table_hbm.1), custom_call_target="tpu_custom_call" | custom-call | tf_op jit(solution)/shard_map/pallas_call | solution.py:550
  3.7 115.1 %shard_map.114 = (s16[6,4,18,32,256]{4,3,2,1,0:T(8,128)(2,1)}, f32[4,32,128,128]{3,2,1,0:T(8,128)}, f32[4,2,16,128]{3,2,1,0:T(8,128)}) custom-call(bf16[2,11,32,128,128]{4,3,2,1,0:T(8,128)(2,1)} %rec_hbm.1, bf16[6,96,1024]{2,1,0:T(8,128)(2,1)} %shard_map.113.own_hbm, bf16[4,2,208,192]{3,2,1,0:T(8,128)(2,1)} %constant.14.clone.tza_hbm, ...), custom_call_target="tpu_custom_call" | custom-call | flops 35999997952 | bytes 30000000 | tf_op jit(solution)/shard_map/pallas_call | solution.py:565
  118.8 11.3 %shard_map.115 = (f32[6,32,128,128]{3,2,1,0:T(8,128)}, f32[2,2,16,128]{3,2,1,0:T(8,128)}) custom-call(s16[6,4,18,32,256]{4,3,2,1,0:T(8,128)(2,1)} %get-tuple-element.7.blocks_ref, f32[4,32,128,128]{3,2,1,0:T(8,128)} %get-tuple-element.8.early_hbm, bf16[768,256]{1,0:T(8,128)(2,1)} %constant.20.clone.ty_ref, bf16[128,480]{1,0:T(8,128)(2,1)} %constant.19.clone.tb_ref.tz_ref), custom_call_target="tpu_custom_call" | custom-call | flops 2000000000 | bytes 20000000 | tf_op jit(solution)/shard_map/pallas_call | solution.py:610
  130.2 5.1 %shard_map.116 = f32[1,6]{1,0:T(1,128)} custom-call(f32[4,2,16,128]{3,2,1,0:T(8,128)} %get-tuple-element.10.first_ref, f32[2,2,16,128]{3,2,1,0:T(8,128)} %get-tuple-element.11.last_ref), custom_call_target="tpu_custom_call" | custom-call | tf_op jit(solution)/shard_map/pallas_call | solution.py:635
  135.3 1.1 copy.13

commit v6 on v5

--- a/solution.py
+++ b/solution.py
@@ -320,6 +320,7 @@
     lax.fori_loop(0, lane_groups, first, 0)
 
     parts = xs // width
+    early = 2 * (rotations // 2) - 3
 
     def load_block(f, h):
         return pltpu.make_async_copy(recv_hbm.at[f, :, :, pl.ds(h * width, width)], blocks.at[h], in_sem.at[h])
@@ -347,7 +348,7 @@
     def rotation_pair(p, carry):
         forward(2 * p, even_re, even_im, odd_re, odd_im)
         forward(2 * p + 1, odd_re, odd_im, even_re, even_im)
-        lax.fori_loop(jnp.maximum(2 * p - 2, 0), 2 * p, end, 0)
+        lax.fori_loop(jnp.maximum(2 * p - 2, 0), jnp.minimum(2 * p, early), end, 0)
         return carry
 
     lax.fori_loop(0, rotations // 2, rotation_pair, 0)
@@ -355,7 +356,6 @@
         forward(rotations - 1, even_re, even_im, odd_re, odd_im)
     for r in range(max(rotations - 2, 0), rotations):
         release(r)
-    early = 2 * (rotations // 2) - 2
     for h in range(parts):
         store_block(early - 1, h).wait()
 
@@ -560,7 +560,7 @@
 
     width = min(16, xs)
     parts = xs // width
-    early = 2 * (rotations // 2) - 2
+    early = 2 * (rotations // 2) - 3
     late = rotations - early
     sent, early_scores, early_lows = pl.pallas_call(
         functools.partial(main_kernel, channels, planes, box, groups, rotations, length, cuts, tops, width, terms),

time: 137 us -> 137 us (level)
    pallas_call x1, Pallas kernels: 115 us -> 113 us  [shards(): pl.pallas_call(functools.partial(main_kernel, channels, planes, box, grou...]
    pallas_call x1, Pallas kernels: 11.3 us -> 13.3 us  [shards(): pl.pallas_call(functools.partial(final_kernel, groups, planes, length, wi...]
where the time goes in v6:
time: 137 us; the launch traced here: 136 us
  Pallas kernels  134 us (98%)
    pallas_call x1, Pallas kernels, shards(): pl.pallas_call(functools.partial(main_kernel, channels, planes, box, grou...  113 us
    pallas_call x1, Pallas kernels, shards(): pl.pallas_call(functools.partial(final_kernel, groups, planes, length, wi...  13.3 us
    pallas_call x1, Pallas kernels, shards(): pl.pallas_call(functools.partial(best_kernel, groups, rotations, early),...  5.12 us
    pallas_call x1, Pallas kernels, shards(): pl.pallas_call(functools.partial(pick_kernel, cuts), in_specs=[pl.BlockSp...  3.04 us

profile of v6, /device:TPU:0, one launch (start us, length us, event | category | flops | bytes accessed | tf_op | source)
XLA Modules:
  0.0 136.2 jit_solution(17601068639896905380)
XLA Ops:
  0.6 3.0 %shard_map.113.own_hbm = bf16[6,96,1024]{2,1,0:T(8,128)(2,1)} custom-call(s32[6]{0:T(128)} %index_ref.1, bf16[32,11,8,1024]{3,2,1,0:T(8,128)(2,1)} %table_hbm.1), custom_call_target="tpu_custom_call" | custom-call | tf_op jit(solution)/shard_map/pallas_call | solution.py:550
  3.7 112.9 %shard_map.114 = (s16[6,4,18,32,256]{4,3,2,1,0:T(8,128)(2,1)}, f32[3,32,128,128]{3,2,1,0:T(8,128)}, f32[3,2,16,128]{3,2,1,0:T(8,128)}) custom-call(bf16[2,11,32,128,128]{4,3,2,1,0:T(8,128)(2,1)} %rec_hbm.1, bf16[6,96,1024]{2,1,0:T(8,128)(2,1)} %shard_map.113.own_hbm, bf16[4,2,208,192]{3,2,1,0:T(8,128)(2,1)} %constant.14.clone.tza_hbm, ...), custom_call_target="tpu_custom_call" | custom-call | flops 35999997952 | bytes 30000000 | tf_op jit(solution)/shard_map/pallas_call | solution.py:565
  116.6 13.3 %shard_map.115 = (f32[6,32,128,128]{3,2,1,0:T(8,128)}, f32[3,2,16,128]{3,2,1,0:T(8,128)}) custom-call(s16[6,4,18,32,256]{4,3,2,1,0:T(8,128)(2,1)} %get-tuple-element.7.blocks_ref, f32[3,32,128,128]{3,2,1,0:T(8,128)} %get-tuple-element.8.early_hbm, bf16[768,256]{1,0:T(8,128)(2,1)} %constant.20.clone.ty_ref, bf16[128,480]{1,0:T(8,128)(2,1)} %constant.19.clone.tb_ref.tz_ref), custom_call_target="tpu_custom_call" | custom-call | flops 3000000000 | bytes 20000000 | tf_op jit(solution)/shard_map/pallas_call | solution.py:610
  129.9 5.1 %shard_map.116 = f32[1,6]{1,0:T(1,128)} custom-call(f32[3,2,16,128]{3,2,1,0:T(8,128)} %get-tuple-element.10.first_ref, f32[3,2,16,128]{3,2,1,0:T(8,128)} %get-tuple-element.11.last_ref), custom_call_target="tpu_custom_call" | custom-call | tf_op jit(solution)/shard_map/pallas_call | solution.py:635
  135.1 1.1 copy.13
